TPU v7x, 256 devices: a whole 4x4x8 slice. The times are simulated.
256 devices in a mesh: seq: 32 (over y, x, core), exp: 8 (over z).
Axes of the slice: x: 4, y: 4, z: 8, core: 2. Of those that a mesh axis runs over, the one named last changes fastest.
Arguments:
- queries: bfloat16 [32768, 2048], P('seq', 'exp'), may hold values from -6 to 6
- keys: bfloat16 [32768, 2048], P('seq', 'exp'), may hold values from -6 to 6
- values: bfloat16 [32768, 2048], P('seq', 'exp'), may hold values from -6 to 6
- out_gate: bfloat16 [32768, 2048], P('seq', 'exp'), may hold values from -6 to 6
- decay_log: float32 [32768, 2048], P('seq', 'exp'), may hold values from -0.86 to 0
- beta: float32 [16, 32768], P('exp', 'seq'), may hold values from 0.0005 to 0.98
- w_out: bfloat16 [2048, 1152], P('exp'), may hold values from -0.125 to 0.125
- resid: bfloat16 [32768, 1152], P(('seq', 'exp')), may hold values from -6 to 6
- norm_gain: float32 [1152], replicated, may hold values from 0.1 to 1.9
- router: bfloat16 [1152, 256], replicated, may hold values from -0.1875 to 0.1875
- w_gate_up: bfloat16 [256, 1152, 2048], P(('seq', 'exp')), may hold values from -0.1875 to 0.1875
- w_down: bfloat16 [256, 1024, 1152], P(('seq', 'exp')), may hold values from -0.1875 to 0.1875
- block_experts: int32 [256, 8], replicated, may hold values from 0 to 255, as said below
Outputs:
- moe_out: bfloat16 [32768, 1152], P(('seq', 'exp'))
Inputs may be any that keep to these rules, and one draw needn't show every extreme that they name: `block_experts`: expert e is counted as row e // 8 and column e % 8; slot j of every block names an expert of column j % 8. `block_experts`: for every seq index s and column c, the 8 slots of column c in blocks s * 8 to s * 8 + 7 name experts of 8 different rows. `block_experts`: every expert is named by 1 to 14 slots of the whole batch, and some expert by exactly 14.
All inputs are finite; a program needn't handle non-finite values.
Results may differ from a plain program's by a relative error of at most 0.023.
Values may be sent and summed in bfloat16 or wider, within the bound.
A program may use at most 128 MiB of HBM per device.

v0:
```python
import jax
import jax.numpy as jnp
from jax import lax
from jax.sharding import PartitionSpec as P

DK = 128
TOPK = 8
SPAN = 64


precise = lax.Precision.HIGHEST
route_scale = 2.446
epsilon = 1e-06


def passed_along(block, axis, distance):
    devices = range(lax.axis_size(axis))
    route = [(i - distance, i) for i in devices if i - distance in devices]
    return lax.ppermute(block, axis, route)


def unit_rows(array):
    return array * lax.rsqrt(jnp.sum(array * array, axis=-1, keepdims=True) + epsilon)


def span_terms(query_heads, key_heads, value_heads, log_rates, betas):
    log_decay = jnp.cumsum(log_rates, axis=2)
    log_last = log_decay[:, :, -1:, :]
    query_hat = query_heads * jnp.exp(log_decay)
    key_hat = key_heads * jnp.exp(log_decay)
    key_inv = key_heads * jnp.exp(-log_decay)
    key_end = key_heads * jnp.exp(log_last - log_decay)
    span_len = query_heads.shape[2]
    key_width = query_heads.shape[3]
    strict = jnp.tril(jnp.ones((span_len, span_len), jnp.float32), -1)
    within = jnp.tril(jnp.ones((span_len, span_len), jnp.float32))
    key_pairs = jnp.einsum("hnid,hnjd->hnij", key_hat, key_inv, precision=precise)
    system = jnp.eye(span_len, dtype=jnp.float32) + betas[..., None] * key_pairs * strict
    right_side = jnp.concatenate(
        [betas[..., None] * value_heads, betas[..., None] * key_hat], axis=-1
    )
    solved = jax.scipy.linalg.solve_triangular(system, right_side, lower=True, unit_diagonal=True)
    value_width = value_heads.shape[-1]
    base_vals = solved[..., :value_width]
    key_solve = solved[..., value_width:]
    scores = jnp.einsum("hnid,hnjd->hnij", query_hat, key_inv, precision=precise) * within
    local_out = jnp.einsum("hnij,hnje->hnie", scores, base_vals, precision=precise)
    query_carry = query_hat - jnp.einsum("hnij,hnjd->hnid", scores, key_solve, precision=precise)
    transit = jnp.exp(log_last[:, :, 0, :])[..., :, None] * jnp.eye(key_width, dtype=jnp.float32)
    transit = transit - jnp.einsum("hnjd,hnje->hnde", key_end, key_solve, precision=precise)
    offset = jnp.einsum("hnjd,hnje->hnde", key_end, base_vals, precision=precise)
    return (local_out, query_carry, transit, offset)


def compose(carry, span):
    device_map, device_shift = carry
    transit, offset = span
    next_map = jnp.einsum("hij,hjk->hik", transit, device_map, precision=precise)
    next_shift = jnp.einsum("hij,hjk->hik", transit, device_shift, precision=precise) + offset
    return ((next_map, next_shift), None)


def advance(state, span):
    local_out, query_carry, transit, offset = span
    output = local_out + jnp.einsum("hid,hde->hie", query_carry, state, precision=precise)
    state = jnp.einsum("hij,hjk->hik", transit, state, precision=precise) + offset
    return (state, output)


def local(
    queries,
    keys,
    values,
    out_gate,
    decay_log,
    beta,
    w_out,
    resid,
    norm_gain,
    router,
    w_gate_up,
    w_down,
    block_experts,
):
    seq_count = lax.axis_size("seq")
    exp_count = lax.axis_size("exp")
    seq_rows = queries.shape[0]
    heads_here = queries.shape[1] // DK
    span_count = seq_rows // SPAN

    def split_heads(array):
        return jnp.moveaxis(
            array.astype(jnp.float32).reshape(span_count, SPAN, heads_here, DK), 2, 0
        )

    query_heads = unit_rows(split_heads(queries))
    key_heads = unit_rows(split_heads(keys))
    value_heads = split_heads(values)
    rate_heads = split_heads(decay_log)
    beta_heads = beta.reshape(heads_here, span_count, SPAN)
    local_out, query_carry, transit, offset = span_terms(
        query_heads, key_heads, value_heads, rate_heads, beta_heads
    )
    transit_seq = jnp.moveaxis(transit, 1, 0)
    offset_seq = jnp.moveaxis(offset, 1, 0)
    eye_heads = jnp.broadcast_to(jnp.eye(DK, dtype=jnp.float32), (heads_here, DK, DK))
    zero_state = jnp.zeros((heads_here, DK, DK), jnp.float32)
    (device_map, device_shift), _ = lax.scan(
        compose, (eye_heads, zero_state), (transit_seq, offset_seq)
    )

    def relay_state(hop_index, entering):
        leaving = jnp.einsum("hij,hjk->hik", device_map, entering, precision=precise) + device_shift
        return passed_along(leaving.astype(jnp.bfloat16), "seq", 1).astype(leaving.dtype)

    arriving = lax.fori_loop(0, seq_count - 1, relay_state, zero_state)
    _, outputs = lax.scan(
        advance,
        arriving,
        (jnp.moveaxis(local_out, 1, 0), jnp.moveaxis(query_carry, 1, 0), transit_seq, offset_seq),
    )
    head_out = jnp.moveaxis(outputs, 1, 2).reshape(seq_rows, heads_here, DK)
    scaled = head_out * lax.rsqrt(jnp.mean(head_out * head_out, axis=-1, keepdims=True) + epsilon)
    gated_heads = scaled * jax.nn.sigmoid(
        out_gate.astype(jnp.float32).reshape(seq_rows, heads_here, DK)
    )
    mixed_heads = gated_heads.reshape(seq_rows, heads_here * DK).astype(jnp.bfloat16)
    tok_rows = resid.shape[0]
    model_width = resid.shape[1]
    attn_part = lax.psum_scatter(
        jnp.dot(mixed_heads, w_out, preferred_element_type=jnp.float32).astype(jnp.bfloat16),
        "exp",
        scatter_dimension=0,
        tiled=True,
    ).astype(jnp.float32)
    hidden_state = resid.astype(jnp.float32) + attn_part
    normed = (
        hidden_state
        * lax.rsqrt(jnp.mean(hidden_state * hidden_state, axis=-1, keepdims=True) + epsilon)
        * norm_gain
    ).astype(jnp.bfloat16)
    seq_index = lax.axis_index("seq")
    exp_index = lax.axis_index("exp")
    per_column = TOPK // exp_count
    capacity = 2 * min(TOPK - 1, seq_count // 2)
    layout = block_experts.reshape(seq_count, exp_count, per_column, exp_count)
    column_pick = jnp.arange(exp_count) == exp_index
    row_blocks = lax.all_gather(normed, "exp", axis=0, tiled=True).reshape(
        exp_count, tok_rows, model_width
    )
    own_table = lax.dynamic_index_in_dim(layout, seq_index, 0, keepdims=False)
    sent_experts = jnp.sum(jnp.where(column_pick, own_table, 0), axis=2).reshape(TOPK)
    dest_rows = sent_experts // exp_count
    row_match = dest_rows[None, :] == jnp.arange(seq_count)[:, None]
    copy_block = jnp.arange(TOPK) // per_column
    source_block = jnp.sum(jnp.where(row_match, copy_block[None, :], 0), axis=1)
    outgoing = jnp.take(row_blocks, source_block, axis=0)
    my_expert = seq_index * exp_count + exp_index
    column_experts = jnp.sum(jnp.where(column_pick, layout, 0), axis=3)
    present = jnp.any(column_experts == my_expert, axis=(1, 2))
    slot_rank = jnp.cumsum(present.astype(jnp.int32)) - 1
    slot_hit = present[None, :] & (slot_rank[None, :] == jnp.arange(capacity)[:, None])
    pick_rows = jnp.sum(jnp.where(slot_hit, jnp.arange(seq_count)[None, :], 0), axis=1)
    hidden_width = w_down.shape[1]
    incoming_blocks = lax.all_to_all(outgoing, "seq", split_axis=0, concat_axis=0, tiled=True)
    packed_blocks = jnp.take(incoming_blocks, pick_rows, axis=0)
    rows_here = packed_blocks.shape[1]
    packed = packed_blocks.reshape(capacity * rows_here, model_width)
    gate_up = jnp.dot(packed, w_gate_up[0], preferred_element_type=jnp.float32)
    expert_hidden = (jax.nn.silu(gate_up[:, :hidden_width]) * gate_up[:, hidden_width:]).astype(
        jnp.bfloat16
    )
    expert_out = jnp.dot(expert_hidden, w_down[0], preferred_element_type=jnp.float32).astype(
        jnp.bfloat16
    )
    expert_out = expert_out.reshape(capacity, rows_here, model_width)
    returned = lax.all_to_all(
        jnp.take(expert_out, jnp.maximum(slot_rank, 0), axis=0),
        "seq",
        split_axis=0,
        concat_axis=0,
        tiled=True,
    )
    per_copy = jnp.take(returned, dest_rows, axis=0).reshape(
        exp_count, per_column, tok_rows, model_width
    )
    collected = lax.all_to_all(per_copy, "exp", split_axis=0, concat_axis=0, tiled=True).reshape(
        TOPK, tok_rows, model_width
    )
    my_ids = lax.dynamic_index_in_dim(block_experts, my_expert, 0, keepdims=False)
    ordered_ids = my_ids.reshape(per_column, exp_count).T.reshape(TOPK)
    router_cols = jnp.take(router, ordered_ids, axis=1)
    scores = jax.nn.sigmoid(jnp.dot(normed, router_cols, preferred_element_type=jnp.float32))
    gate_weights = route_scale * scores / jnp.sum(scores, axis=1, keepdims=True)
    combined = jnp.sum(gate_weights.T[:, :, None] * collected.astype(jnp.float32), axis=0)
    return (hidden_state + combined).astype(jnp.bfloat16)


def solution(mesh):
    return jax.shard_map(
        local,
        mesh=mesh,
        in_specs=(
            P("seq", "exp"),
            P("seq", "exp"),
            P("seq", "exp"),
            P("seq", "exp"),
            P("seq", "exp"),
            P("exp", "seq"),
            P("exp", None),
            P(("seq", "exp"), None),
            P(),
            P(),
            P(("seq", "exp"), None, None),
            P(("seq", "exp"), None, None),
            P(),
        ),
        out_specs=P(("seq", "exp"), None),
        check_vma=False,
    )
```

profile of v0, /device:TPU:66, one launch (start us, length us, event | category | flops | bytes accessed | tf_op | source)
XLA Modules:
  0.0 1031.7 jit_solution(142274380712668025)
XLA Ops:
  29.0 5.0 fusion.39
  34.1 158.7 %custom-call.4 = f32[2,16,1,64,64]{3,4,2,1,0:T(8,128)} custom-call(f32[2,16,1,64,64]{4,3,2,1,0:T(8,128)} %fusion.39), custom_call_target="InvertDiagBlocksLowerTriangular" | custom-call | tf_op jit(solution)/shard_map/jit(_solve_triangular)/vmap(vmap())/triangular_solve | solution.py:42
  205.2 4.0 convolution_bitcast_fusion
  210.7 4.6 bitcast_subtract_fusion
  216.8 39.7 %while.37 = (s32[]{:T(128)}, f32[2,128,128]{2,1,0:T(8,128)S(1)}, f32[2,128,128]{2,1,0:T(8,128)S(1)}, f32[16,2,128,128]{3,2,1,0:T(8,128)}, f32[16,2,128,128]{3,2,1,0:T(8,128)}, /*index=5*/s32[]{:T(128)}, s32[]{:T(128)}) while((s32[]{:T(128)}, f32[2,128,128]{2,1,0:T(8,128)S(1)}, f32[2,128,128]{2,1,0:T(8,128)S(1)}, ...), condition=%wide.region_3.4_spmd.clone, body=%wide.region_2.0_spmd.clone.sunk | while | flops 100728832 | bytes 1443426 | solution.py:108
  256.5 224.5 %while.38 = (s32[]{:T(128)}, f32[2,128,128]{2,1,0:T(8,128)S(1)}, f32[2,128,128]{2,1,0:T(8,128)S(1)}, f32[2,128,128]{2,1,0:T(8,128)S(1)}, s32[]{:T(128)}, /*index=5*/s32[]{:T(128)}) while((s32[]{:T(128)}, f32[2,128,128]{2,1,0:T(8,128)S(1)}, f32[2,128,128]{2,1,0:T(8,128)S(1)}, f32[2,128,128]{2,1,0:T(8,128)S(1)}, s32[]{:T(128)}, ...), condition=%wide.region_5.6_spmd.clone, body=%wide.region_4.5_spmd.clone.sunk | while | flops 50462720 | bytes 917623 | solution.py:116
  258.7 3.7 collective-permute-done
  264.6 3.7 collective-permute-done
  270.5 3.7 collective-permute-done
  315.8 4.3 collective-permute-start
  321.7 6.4 collective-permute-start
  329.3 6.8 collective-permute-start
  337.3 6.8 collective-permute-start
  345.3 6.8 collective-permute-start
  353.3 6.8 collective-permute-start
  361.3 6.8 collective-permute-start
  369.3 6.8 collective-permute-start
  377.3 6.8 collective-permute-start
  385.3 6.8 collective-permute-start
  393.3 6.8 collective-permute-start
  401.3 6.8 collective-permute-start
  409.3 6.8 collective-permute-start
  417.3 6.8 collective-permute-start
  425.3 6.8 collective-permute-start
  433.3 6.8 collective-permute-start
  441.3 6.8 collective-permute-start
  449.3 6.8 collective-permute-start
  457.4 6.8 collective-permute-start
  465.4 6.8 collective-permute-start
  473.4 6.8 collective-permute-start
  481.1 48.2 %while.36 = (s32[]{:T(128)}, f32[2,128,128]{2,1,0:T(8,128)S(1)}, f32[16,2,64,128]{3,2,1,0:T(8,128)}, f32[16,2,128,128]{3,2,1,0:T(8,128)}, f32[16,2,128,128]{3,2,...) while((s32[]{:T(128)}, f32[2,128,128]{2,1,0:T(8,128)S(1)}, ...), condition=%wide.region_8.9_spmd, body=%wide.region_7.8_spmd.sunk | while | flops 75546624 | bytes 1116253 | solution.py:117
  534.5 3.7 convolution_convert_fusion.1
  538.2 65.3 %reduce-scatter.2.cloned.1.call-done = bf16[128,1152]{1,0:T(8,128)(2,1)} async-done(((bf16[1024,1152]{1,0:T(8,128)(2,1)}), bf16[128,1152]{1,0:T(8,128)(2,1)}) %reduce-scatter.2.cloned.1.call-update) | async-done | bytes 294928 | tf_op jit(solution)/shard_map/reduce_scatter | solution.py:130
  607.1 40.6 %all-gather.2.cloned.1.call-done = bf16[1024,1152]{1,0:T(8,128)(2,1)} async-done(((bf16[128,1152]{1,0:T(8,128)(2,1)}), bf16[1024,1152]{1,0:T(8,128)(2,1)}) %all-gather.2.cloned.1.call-update) | async-done | bytes 2359312 | tf_op jit(solution)/shard_map/all_gather | solution.py:148
  647.8 7.1 gather_fusion.1
  654.9 8.3 broadcast_select_fusion
  663.2 7.8 all-to-all-start
  671.9 110.9 %all-to-all-done = bf16[32,128,1152]{2,1,0:T(8,128)(2,1)} async-done(((bf16[32,128,1152]{2,1,0:T(8,128)(2,1)}), bf16[32,128,1152]{2,1,0:T(8,128)(2,1)}, u32[]{:S(2)}, u32[]{:S(2)}) %all-to-all-start) | async-done | bytes 9437216 | tf_op jit(solution)/shard_map/all_to_all | solution.py:165
  782.7 6.9 gather_fusion.2
  792.3 11.8 %fusion.26 = f32[1792,2048]{1,0:T(8,128)S(1)} fusion(bf16[1792,1152]{1,0:T(8,128)(2,1)S(1)} %bitcast.183, bf16[1,1152,2048]{2,1,0:T(8,128)(2,1)} %param.29), kind=kOutput, calls=%fused_computation.40 | convolution fusion | flops 8455716864 | bytes 23527424 | tf_op jit(solution)/shard_map/dot_general | solution.py:169
  804.1 7.4 convolution_convert_fusion
  811.6 7.8 gather_fusion.3
  819.4 8.3 broadcast_select_fusion.1
  827.8 12.1 %all-to-all-start.1 = ((bf16[32,128,1152]{2,1,0:T(8,128)(2,1)}), bf16[32,128,1152]{2,1,0:T(8,128)(2,1)}, u32[]{:S(2)}, u32[]{:S(2)}) async-start(bf16[32,128,1152]{2,1,0:T(8,128)(2,1)} %broadcast_select_fusion.1), calls=%async_computation.2 | async-start | bytes 18874368 | tf_op jit(solution)/shard_map/all_to_all | solution.py:177
  839.9 111.9 %all-to-all-done.1 = bf16[32,128,1152]{2,1,0:T(8,128)(2,1)} async-done(((bf16[32,128,1152]{2,1,0:T(8,128)(2,1)}), bf16[32,128,1152]{2,1,0:T(8,128)(2,1)}, u32[]{:S(2)}, u32[]{:S(2)}) %all-to-all-start.1) | async-done | bytes 9437216 | tf_op jit(solution)/shard_map/all_to_all | solution.py:177
  951.8 5.9 gather_fusion.4
  961.1 5.7 all-to-all-start.2
  970.1 50.4 %all-to-all-done.2 = bf16[8,1,128,1152]{3,2,1,0:T(8,128)(2,1)} async-done(((bf16[8,1,128,1152]{3,2,1,0:T(8,128)(2,1)}), bf16[8,1,128,1152]{3,2,1,0:T(8,128)(2,1)}, u32[]{:S(2)}, u32[]{:S(2)}) %all-to-all-start.2) | async-done | bytes 2359328 | tf_op jit(solution)/shard_map/all_to_all | solution.py:187
  (319 shorter events, 219.8 us)
Async XLA Ops:
  6.5 797.6 %copy-start = (bf16[1,1024,1152]{2,1,0:T(8,128)(2,1)S(1)}, bf16[1,1024,1152]{2,1,0:T(8,128)(2,1)}, u32[]{:S(2)}) copy-start(bf16[1,1024,1152]{2,1,0:T(8,128)(2,1)} %param.30) | copy-start | bytes 7077892
  6.5 8.5 copy-start.14
  6.5 597.0 %reduce-scatter.2.cloned.1.call-start = ((), (), s32[]{:S(2)}) async-start(), calls=%async_computation.4 | async-start | bytes 2654208 | tf_op jit(solution)/shard_map/reduce_scatter | solution.py:130
  192.8 3.0 copy-start.8
  192.8 3.0 copy-start.11
  192.8 5.5 copy-start.5
  198.3 4.3 copy-start.9
  200.3 4.9 copy-start.7
  205.2 5.5 copy-start.6
  205.2 5.5 copy-start.10
  256.8 5.6 collective-permute-start
  262.7 5.6 collective-permute-start
  268.6 5.6 collective-permute-start
  274.5 5.6 collective-permute-start
  280.4 5.6 collective-permute-start
  286.3 5.6 collective-permute-start
  292.2 5.6 collective-permute-start
  298.1 5.6 collective-permute-start
  304.0 5.6 collective-permute-start
  309.9 5.6 collective-permute-start
  315.8 5.6 collective-permute-start
  321.7 7.3 collective-permute-start
  329.3 7.7 collective-permute-start
  337.3 7.7 collective-permute-start
  345.3 7.7 collective-permute-start
  353.3 7.7 collective-permute-start
  361.3 7.7 collective-permute-start
  369.3 7.7 collective-permute-start
  377.3 7.7 collective-permute-start
  385.3 7.7 collective-permute-start
  393.3 7.7 collective-permute-start
  401.3 7.7 collective-permute-start
  409.3 7.7 collective-permute-start
  417.3 7.7 collective-permute-start
  425.3 7.7 collective-permute-start
  433.3 7.7 collective-permute-start
  441.3 7.7 collective-permute-start
  449.3 7.7 collective-permute-start
  457.4 7.7 collective-permute-start
  465.4 7.7 collective-permute-start
  473.4 7.7 collective-permute-start
  534.4 69.1 %copy-start.4 = (bf16[128,1152]{1,0:T(8,128)(2,1)S(1)}, bf16[128,1152]{1,0:T(8,128)(2,1)}, u32[]{:S(2)}) copy-start(bf16[128,1152]{1,0:T(8,128)(2,1)} %param.26) | copy-start | bytes 884740
  534.4 70.3 %copy-start.13 = (f32[1152]{0:T(1024)S(1)}, f32[1152]{0:T(1024)}, u32[]{:S(2)}) copy-start(f32[1152]{0:T(1024)} %param.27) | copy-start | bytes 13828
  534.4 72.1 %copy-start.12 = (s32[256,8]{0,1:T(8,128)S(1)}, s32[256,8]{0,1:T(8,128)}, u32[]{:S(2)}) copy-start(s32[256,8]{0,1:T(8,128)} %param.31) | copy-start | bytes 24580
  538.2 109.6 %all-gather.2.cloned.1.call-start = ((), (), s32[]{:S(2)}) async-start(), calls=%async_computation.5 | async-start | bytes 2654208 | tf_op jit(solution)/shard_map/all_gather | solution.py:148
  663.2 119.5 %all-to-all-start = ((bf16[32,128,1152]{2,1,0:T(8,128)(2,1)}), bf16[32,128,1152]{2,1,0:T(8,128)(2,1)}, u32[]{:S(2)}, u32[]{:S(2)}) async-start(bf16[32,128,1152]{2,1,0:T(8,128)(2,1)} %broadcast_select_fusion), calls=%async_computation.1 | async-start | bytes 18874368 | tf_op jit(solution)/shard_map/all_to_all | solution.py:165
  827.8 124.0 %all-to-all-start.1 = ((bf16[32,128,1152]{2,1,0:T(8,128)(2,1)}), bf16[32,128,1152]{2,1,0:T(8,128)(2,1)}, u32[]{:S(2)}, u32[]{:S(2)}) async-start(bf16[32,128,1152]{2,1,0:T(8,128)(2,1)} %broadcast_select_fusion.1), calls=%async_computation.2 | async-start | bytes 18874368 | tf_op jit(solution)/shard_map/all_to_all | solution.py:177
  961.1 59.5 %all-to-all-start.2 = ((bf16[8,1,128,1152]{3,2,1,0:T(8,128)(2,1)}), bf16[8,1,128,1152]{3,2,1,0:T(8,128)(2,1)}, u32[]{:S(2)}, u32[]{:S(2)}) async-start(bf16[8,1,128,1152]{3,2,1,0:T(8,128)(2,1)} %bitcast_select_fusion), calls=%async_computation.3 | async-start | bytes 4718592 | tf_op jit(solution)/shard_map/all_to_all | solution.py:187
  (3 other events, 7.5 us)
Sparse Core Ops, SparseCore 0:
  538.3 65.2 reduce-scatter.1
  606.7 41.0 all-gather.1
where the time goes:
time: 1050 us; the launch traced here: 1030 us
  waiting for transfers between devices  434 us (41%)
  other arithmetic  204 us (19%)
  starting transfers between devices  185 us (18%)
  matrix products  142 us (14%)
  local copies, waits for them, and re-layouts  49.6 us (5%)
  between operations  14.1 us (1%)
    another operation x4, other arithmetic, span_terms(): jax.scipy.linalg.solve_triangular(system, right_side, lower=True, unit_di...  160 us
    ppermute x31, starting transfers between devices, passed_along(): return lax.ppermute(block, axis, route)  160 us
    all_to_all x1, waiting for transfers between devices, local(): lax.all_to_all(jnp.take(expert_out, jnp.maximum(slot_rank, 0), axis=0), '...  112 us
    all_to_all x1, waiting for transfers between devices, local(): lax.all_to_all(outgoing, 'seq', split_axis=0, concat_axis=0, tiled=True)  111 us
    reduce_scatter x1, waiting for transfers between devices, local(): lax.psum_scatter(jnp.dot(mixed_heads, w_out, preferred_element_type=jnp.f...  65.3 us
    ppermute x31, waiting for transfers between devices, passed_along(): return lax.ppermute(block, axis, route)  55.1 us
    all_to_all x1, waiting for transfers between devices, local(): lax.all_to_all(per_copy, 'exp', split_axis=0, concat_axis=0, tiled=True)  50.4 us
    all_gather x1, waiting for transfers between devices, local(): lax.all_gather(normed, 'exp', axis=0, tiled=True)  40.6 us
  transfers between devices with their start and end apart: 36, of which 36 were waited for; matrix products, arithmetic and copies ran while one was open for 0% of the time, Pallas kernels for 0%

commit v1 on v0

v1 whole, which is shorter than its diff:
```python
import functools

import jax
import jax.numpy as jnp
from jax import lax
from jax.experimental import pallas as pl
from jax.experimental.pallas import tpu as pltpu
from jax.sharding import PartitionSpec as P

DK = 128
TOPK = 8
CH = 64
PAIR = 128
STEP = 256
NEAR = 8
FAR = 4
F32, BF16 = jnp.float32, jnp.bfloat16
MESH = pl.DeviceIdType.MESH
NN = (((1,), (0,)), ((), ()))
NT = (((1,), (1,)), ((), ()))
TN = (((0,), (0,)), ((), ()))

route_scale = 2.446
epsilon = 1e-06


def split(a):
    high = a.astype(BF16)
    return high, (a - high.astype(F32)).astype(BF16)


def mm(a, b, dims=NN):
    return lax.dot_general(a, b, dims, preferred_element_type=F32)


def dot1(a, b, dims=NN):
    return mm(a.astype(BF16), b.astype(BF16), dims)


def dot3(a, b, dims=NN):
    ah, al = split(a)
    bh, bl = split(b)
    return mm(ah, bh, dims) + (mm(ah, bl, dims) + mm(al, bh, dims))


def unit(x):
    return x * lax.rsqrt(jnp.sum(x * x, axis=-1, keepdims=True) + epsilon)


def delta_kernel(q_ref, k_ref, v_ref, d_ref, b_ref, qo_ref, oo_ref, mb_ref, state):
    heads = q_ref.shape[1] // 128
    step = pl.program_id(0)
    row = lax.broadcasted_iota(jnp.int32, (PAIR, PAIR), 0)
    col = lax.broadcasted_iota(jnp.int32, (PAIR, PAIR), 1)

    @pl.when(step == 0)
    def _():
        eye = jnp.where(row == col, 1.0, 0.0).astype(F32)
        for h in range(heads):
            state[h, :, :128] = eye
            state[h, :, 128:] = jnp.zeros((128, 128), F32)

    same = (row // CH) == (col // CH)
    incl = same & (col <= row)
    strict = same & (col < row)
    tri = jnp.where(incl, 1.0, 0.0).astype(BF16)
    eye = jnp.where(row == col, 1.0, 0.0).astype(F32)
    work = {}
    for p in range(STEP // PAIR):
        rows = pl.ds(p * PAIR, PAIR)
        log = d_ref[rows, :]
        l1 = log.astype(BF16)
        r1 = log - l1.astype(F32)
        l2 = r1.astype(BF16)
        l3 = (r1 - l2.astype(F32)).astype(BF16)
        acc = mm(tri, l1) + (mm(tri, l2) + mm(tri, l3))
        top = lax.broadcasted_iota(jnp.int32, acc.shape, 0) < CH
        last = jnp.where(top, acc[CH - 1 : CH, :], acc[PAIR - 1 : PAIR, :])
        grow = jnp.exp(acc)
        shrink = jnp.exp(-acc)
        tail = jnp.exp(last - acc)
        total = jnp.exp(last)
        for h in range(heads):
            cols = pl.ds(h * 128, 128)
            hs = slice(h * 128, h * 128 + 128)
            key = unit(k_ref[rows, cols].astype(F32))
            query = unit(q_ref[rows, cols].astype(F32))
            beta = b_ref[rows, h : h + 1]
            key_hat = key * grow[:, hs]
            key_inv = key * shrink[:, hs]
            key_end = key * tail[:, hs]
            query_hat = query * grow[:, hs]
            low = jnp.where(strict, dot3(key_hat, key_inv, NT) * beta, 0.0)
            score = jnp.where(incl, dot1(query_hat, key_inv, NT), 0.0)
            inv = eye - jnp.where((row // 2 == col // 2), low, 0.0)
            size = 2
            while size < CH:
                part = jnp.where((row // (2 * size) == col // (2 * size)) & (row // size != col // size), low, 0.0)
                inv = inv - dot3(inv, dot3(part, inv))
                size *= 2
            right = jnp.concatenate([beta * key_hat, beta * v_ref[rows, cols].astype(F32)], axis=1)
            solved = dot3(inv, right)
            work[p, h] = (solved, score, query_hat, key_end, total[:, hs])
    zero = jnp.zeros((CH, 128), F32)
    for h in range(heads):
        cur = state[h]
        for p in range(STEP // PAIR):
            solved, score, query_hat, key_end, total = work[p, h]
            for half in range(2):
                rs = slice(half * CH, half * CH + CH)
                lead = dot3(jnp.concatenate([solved[rs, :128], query_hat[rs]], axis=0), cur)
                upd = jnp.concatenate([zero, solved[rs, 128:]], axis=1) - lead[:CH]
                out = lead[CH:] + dot1(score[rs, rs], upd)
                at = pl.ds(p * PAIR + half * CH, CH)
                qo_ref[at, h * 128 : h * 128 + 128] = out[:, :128].astype(qo_ref.dtype)
                oo_ref[at, h * 128 : h * 128 + 128] = out[:, 128:]
                fade = jnp.transpose(total[half * CH : half * CH + 8, :])[:, :1]
                cur = fade * cur + dot3(key_end[rs], upd, TN)
        state[h] = cur

    @pl.when(step == pl.num_programs(0) - 1)
    def _():
        for h in range(heads):
            mb_ref[h] = state[h].astype(mb_ref.dtype)


def delta(q, k, v, d, bt):
    rows, width = q.shape
    heads = width // 128
    spec = pl.BlockSpec((STEP, width), lambda i: (i, 0))
    return pl.pallas_call(
        delta_kernel,
        grid=(rows // STEP,),
        out_shape=(
            jax.ShapeDtypeStruct((rows, width), BF16),
            jax.ShapeDtypeStruct((rows, width), F32),
            jax.ShapeDtypeStruct((heads, 128, 256), BF16),
        ),
        in_specs=[spec, spec, spec, spec, pl.BlockSpec((STEP, heads), lambda i: (i, 0))],
        out_specs=(spec, spec, pl.BlockSpec((heads, 128, 256), lambda i: (0, 0, 0))),
        scratch_shapes=[pltpu.VMEM((heads, 128, 256), F32)],
        compiler_params=pltpu.CompilerParams(vmem_limit_bytes=40 * 2**20),
        cost_estimate=pl.CostEstimate(flops=5_000_000_000, bytes_accessed=6_000_000, transcendentals=0),
        name="delta_chunks",
    )(q, k, v, d, bt)


def mixer_kernel(
    mb_ref, q_ref, o_ref, gate_ref, resid_ref, gain_ref, w_ref, hidden_ref, normed_ref,
    near, far, total, mixed, mix, wide, near_s, near_r, far_s, far_r, mix_s, mix_r, w_sem,
):
    heads = mb_ref.shape[0]
    seq, exp = lax.axis_index("seq"), lax.axis_index("exp")
    group, slot = seq // NEAR, seq % NEAR
    exps = mix.shape[0]
    rows = normed_ref.shape[0]
    fetch = pltpu.make_async_copy(w_ref, wide, w_sem)
    fetch.start()
    barrier = pltpu.get_barrier_semaphore()
    for d in range(1, NEAR):
        peer = {"seq": group * NEAR + (slot + d) % NEAR}
        pl.semaphore_signal(barrier, inc=1, device_id=peer, device_id_type=MESH)
    for d in range(1, FAR):
        peer = {"seq": ((group + d) % FAR) * NEAR + slot}
        pl.semaphore_signal(barrier, inc=1, device_id=peer, device_id_type=MESH)
    for d in range(1, exps):
        pl.semaphore_signal(barrier, inc=1, device_id={"exp": (exp + d) % exps}, device_id_type=MESH)
    pl.semaphore_wait(barrier, NEAR + FAR + exps - 3)

    def near_copy(peer, place):
        return pltpu.make_async_remote_copy(
            src_ref=mb_ref, dst_ref=near.at[place], send_sem=near_s.at[peer], recv_sem=near_r.at[place],
            device_id={"seq": group * NEAR + peer}, device_id_type=MESH)

    def far_copy(peer, place):
        return pltpu.make_async_remote_copy(
            src_ref=total, dst_ref=far.at[place], send_sem=far_s.at[peer], recv_sem=far_r.at[place],
            device_id={"seq": peer * NEAR + slot}, device_id_type=MESH)

    def mix_copy(peer, place):
        return pltpu.make_async_remote_copy(
            src_ref=mixed.at[peer], dst_ref=mix.at[place], send_sem=mix_s.at[peer], recv_sem=mix_r.at[place],
            device_id={"exp": peer}, device_id_type=MESH)

    for d in range(1, NEAR):
        near_copy((slot + d) % NEAR, slot).start()
    near[slot] = mb_ref[...]
    row = lax.broadcasted_iota(jnp.int32, (128, 256), 0)
    col = lax.broadcasted_iota(jnp.int32, (128, 256), 1)
    start = jnp.where(row == col, 1.0, 0.0).astype(F32)
    shifts = col >= 128

    def apply(block, carried):
        high, low = split(carried)
        lead = block[:, :128]
        return mm(lead, high) + mm(lead, low)

    cur = [start] * heads
    before = [start] * heads
    for j in range(NEAR):
        @pl.when(j != slot)
        def _():
            near_copy(j, j).wait_recv()

        for h in range(heads):
            before[h] = jnp.where(slot == j, cur[h], before[h])
            block = near[j, h]
            cur[h] = apply(block, cur[h]) + jnp.where(shifts, block.astype(F32), 0.0)
    for h in range(heads):
        total[h] = cur[h].astype(BF16)
    for d in range(1, FAR):
        far_copy((group + d) % FAR, group).start()
    far[group] = total[...]
    state = [jnp.zeros((128, 128), F32)] * heads
    for g in range(FAR):
        @pl.when(g != group)
        def _():
            far_copy(g, g).wait_recv()

        for h in range(heads):
            block = far[g, h]
            moved = apply(block, state[h]) + block[:, 128:].astype(F32)
            state[h] = jnp.where(g < group, moved, state[h])
    parts = []
    for h in range(heads):
        entering = dot3(before[h][:, :128], state[h]) + before[h][:, 128:]
        parts.append(split(entering))

    def mix_rows(peer):
        at = pl.ds(pl.multiple_of(peer * rows, rows), rows)
        for h in range(heads):
            cols = pl.ds(h * 128, 128)
            query = q_ref[at, cols]
            out = mm(query, parts[h][0]) + mm(query, parts[h][1]) + o_ref[at, cols]
            out = out * lax.rsqrt(jnp.mean(out * out, axis=-1, keepdims=True) + epsilon)
            gate = gate_ref[at, cols].astype(F32)
            mixed[peer, :, cols] = (out / (1.0 + jnp.exp(-gate))).astype(BF16)

    for d in range(1, exps):
        peer = (exp + d) % exps
        mix_rows(peer)
        mix_copy(peer, exp).start()
    mix_rows(exp)
    mix[exp] = mixed[exp]
    fetch.wait()
    acc = resid_ref[...].astype(F32)
    for d in range(exps):
        source = (exp + exps - d) % exps
        if d:
            mix_copy(source, source).wait_recv()
        wrows = pl.ds(pl.multiple_of(source * 256, 256), 256)
        acc = acc + mm(mix[source], wide[wrows, :])
    hidden_ref[...] = acc
    scale = lax.rsqrt(jnp.mean(acc * acc, axis=-1, keepdims=True) + epsilon)
    normed_ref[...] = (acc * scale * gain_ref[...]).astype(BF16)
    for d in range(1, NEAR):
        near_copy((slot + d) % NEAR, slot).wait_send()
    for d in range(1, FAR):
        far_copy((group + d) % FAR, group).wait_send()
    for d in range(1, exps):
        mix_copy((exp + d) % exps, exp).wait_send()


def mixer(mb, q, o, gate, resid, gain, w_full, exps):
    rows, width = resid.shape
    heads = mb.shape[0]
    vmem = pl.BlockSpec(memory_space=pltpu.VMEM)
    dma = pltpu.SemaphoreType.DMA
    return pl.pallas_call(
        mixer_kernel,
        out_shape=(
            jax.ShapeDtypeStruct((rows, width), F32),
            jax.ShapeDtypeStruct((rows, width), BF16),
        ),
        in_specs=[vmem] * 6 + [pl.BlockSpec(memory_space=pl.ANY)],
        out_specs=(vmem, vmem),
        scratch_shapes=[
            pltpu.VMEM((NEAR, heads, 128, 256), BF16),
            pltpu.VMEM((FAR, heads, 128, 256), BF16),
            pltpu.VMEM((heads, 128, 256), BF16),
            pltpu.VMEM((exps, rows, heads * 128), BF16),
            pltpu.VMEM((exps, rows, heads * 128), BF16),
            pltpu.VMEM(w_full.shape, BF16),
            dma((NEAR,)), dma((NEAR,)), dma((FAR,)), dma((FAR,)), dma((exps,)), dma((exps,)), dma,
        ],
        compiler_params=pltpu.CompilerParams(
            collective_id=0, has_side_effects=True, vmem_limit_bytes=48 * 2**20
        ),
        name="mixer",
    )(mb, q, o, gate, resid, gain, w_full)


def local(
    queries,
    keys,
    values,
    out_gate,
    decay_log,
    beta,
    w_out,
    resid,
    norm_gain,
    router,
    w_gate_up,
    w_down,
    block_experts,
):
    seq_count = lax.axis_size("seq")
    exp_count = lax.axis_size("exp")
    tok_rows, model_width = resid.shape
    w_full = lax.all_gather(w_out, "exp", axis=0, tiled=True)
    q_lead, o_lead, carried = delta(queries, keys, values, decay_log, beta.T)
    hidden_state, normed = mixer(
        carried, q_lead, o_lead, out_gate, resid, norm_gain.reshape(1, -1), w_full, exp_count
    )
    seq_index = lax.axis_index("seq")
    exp_index = lax.axis_index("exp")
    per_column = TOPK // exp_count
    capacity = 2 * min(TOPK - 1, seq_count // 2)
    layout = block_experts.reshape(seq_count, exp_count, per_column, exp_count)
    column_pick = jnp.arange(exp_count) == exp_index
    row_blocks = lax.all_gather(normed, "exp", axis=0, tiled=True).reshape(
        exp_count, tok_rows, model_width
    )
    own_table = lax.dynamic_index_in_dim(layout, seq_index, 0, keepdims=False)
    sent_experts = jnp.sum(jnp.where(column_pick, own_table, 0), axis=2).reshape(TOPK)
    dest_rows = sent_experts // exp_count
    row_match = dest_rows[None, :] == jnp.arange(seq_count)[:, None]
    copy_block = jnp.arange(TOPK) // per_column
    source_block = jnp.sum(jnp.where(row_match, copy_block[None, :], 0), axis=1)
    outgoing = jnp.take(row_blocks, source_block, axis=0)
    my_expert = seq_index * exp_count + exp_index
    column_experts = jnp.sum(jnp.where(column_pick, layout, 0), axis=3)
    present = jnp.any(column_experts == my_expert, axis=(1, 2))
    slot_rank = jnp.cumsum(present.astype(jnp.int32)) - 1
    slot_hit = present[None, :] & (slot_rank[None, :] == jnp.arange(capacity)[:, None])
    pick_rows = jnp.sum(jnp.where(slot_hit, jnp.arange(seq_count)[None, :], 0), axis=1)
    hidden_width = w_down.shape[1]
    incoming_blocks = lax.all_to_all(outgoing, "seq", split_axis=0, concat_axis=0, tiled=True)
    packed_blocks = jnp.take(incoming_blocks, pick_rows, axis=0)
    rows_here = packed_blocks.shape[1]
    packed = packed_blocks.reshape(capacity * rows_here, model_width)
    gate_up = jnp.dot(packed, w_gate_up[0], preferred_element_type=jnp.float32)
    expert_hidden = (jax.nn.silu(gate_up[:, :hidden_width]) * gate_up[:, hidden_width:]).astype(
        jnp.bfloat16
    )
    expert_out = jnp.dot(expert_hidden, w_down[0], preferred_element_type=jnp.float32).astype(
        jnp.bfloat16
    )
    expert_out = expert_out.reshape(capacity, rows_here, model_width)
    returned = lax.all_to_all(
        jnp.take(expert_out, jnp.maximum(slot_rank, 0), axis=0),
        "seq",
        split_axis=0,
        concat_axis=0,
        tiled=True,
    )
    per_copy = jnp.take(returned, dest_rows, axis=0).reshape(
        exp_count, per_column, tok_rows, model_width
    )
    collected = lax.all_to_all(per_copy, "exp", split_axis=0, concat_axis=0, tiled=True).reshape(
        TOPK, tok_rows, model_width
    )
    my_ids = lax.dynamic_index_in_dim(block_experts, my_expert, 0, keepdims=False)
    ordered_ids = my_ids.reshape(per_column, exp_count).T.reshape(TOPK)
    router_cols = jnp.take(router, ordered_ids, axis=1)
    scores = jax.nn.sigmoid(jnp.dot(normed, router_cols, preferred_element_type=jnp.float32))
    gate_weights = route_scale * scores / jnp.sum(scores, axis=1, keepdims=True)
    combined = jnp.sum(gate_weights.T[:, :, None] * collected.astype(jnp.float32), axis=0)
    return (hidden_state + combined).astype(jnp.bfloat16)


def solution(mesh):
    return jax.shard_map(
        local,
        mesh=mesh,
        in_specs=(
            P("seq", "exp"),
            P("seq", "exp"),
            P("seq", "exp"),
            P("seq", "exp"),
            P("seq", "exp"),
            P("exp", "seq"),
            P("exp", None),
            P(("seq", "exp"), None),
            P(),
            P(),
            P(("seq", "exp"), None, None),
            P(("seq", "exp"), None, None),
            P(),
        ),
        out_specs=P(("seq", "exp"), None),
        check_vma=False,
    )
```

time: 1050 us -> 542 us (0.52); the launches traced: 1030 us -> 535 us
  other arithmetic: 204 us -> 25 us
  starting transfers between devices: 185 us -> 25.4 us
  matrix products: 142 us -> 19.5 us
  waiting for transfers between devices: 434 us -> 320 us
  Pallas kernels: 0 us -> 87.3 us
    another operation x6 -> x1, other arithmetic: 161 us -> 0.06 us  [the longest x4 160 us: span_terms(): jax.scipy.linalg.solve_triangular(system, right_side, lower=True, unit_di...]
    ppermute x31 -> x0, starting transfers between devices: 160 us -> none  [passed_along(): return lax.ppermute(block, axis, route)]
    dot_general x102 -> x0, matrix products: 119 us -> none  [the longest x16 27.8 us: advance(): jnp.einsum('hid,hde->hie', query_carry, state, precision=precise)]
    pallas_call x0 -> x2, Pallas kernels: none -> 87.3 us  [the longest x1 44.4 us: delta(): pl.pallas_call(delta_kernel, grid=(rows // STEP,), out_shape=(jax.ShapeDt...]
    reduce_scatter x1 -> x0, waiting for transfers between devices: 65.3 us -> none  [local(): lax.psum_scatter(jnp.dot(mixed_heads, w_out, preferred_element_type=jnp.f...]
    ppermute x31 -> x0, waiting for transfers between devices: 55.1 us -> none  [passed_along(): return lax.ppermute(block, axis, route)]
  transfers between devices with their start and end apart: 36 -> 5, of which waited for: 36 -> 5; matrix products, arithmetic and copies ran while one was open for 0% -> 2% of each run, Pallas kernels for 0% -> 8%
where the time goes in v1:
time: 542 us; the launch traced here: 535 us
  waiting for transfers between devices  320 us (59%)
  Pallas kernels  87.3 us (16%)
  local copies, waits for them, and re-layouts  44.3 us (8%)
  starting transfers between devices  25.4 us (5%)
  other arithmetic  25 us (5%)
  matrix products  19.5 us (4%)
  between operations  13.7 us (3%)
    all_to_all x1, waiting for transfers between devices, local(): lax.all_to_all(jnp.take(expert_out, jnp.maximum(slot_rank, 0), axis=0), '...  112 us
    all_to_all x1, waiting for transfers between devices, local(): lax.all_to_all(outgoing, 'seq', split_axis=0, concat_axis=0, tiled=True)  111 us
    all_to_all x1, waiting for transfers between devices, local(): lax.all_to_all(per_copy, 'exp', split_axis=0, concat_axis=0, tiled=True)  49.3 us
    pallas_call x1, Pallas kernels, delta(): pl.pallas_call(delta_kernel, grid=(rows // STEP,), out_shape=(jax.ShapeDt...  44.4 us
    pallas_call x1, Pallas kernels, mixer(): pl.pallas_call(mixer_kernel, out_shape=(jax.ShapeDtypeStruct((rows, width...  42.8 us
    all_gather x1, waiting for transfers between devices, local(): lax.all_gather(normed, 'exp', axis=0, tiled=True)  38 us
    unnamed x35, local copies, waits for them, and re-layouts  14.9 us
    all_to_all x1, starting transfers between devices, local(): lax.all_to_all(jnp.take(expert_out, jnp.maximum(slot_rank, 0), axis=0), '...  12.3 us
  transfers between devices with their start and end apart: 5, of which 5 were waited for; matrix products, arithmetic and copies ran while one was open for 2% of the time, Pallas kernels for 8%

profile of v1, /device:TPU:66, one launch (start us, length us, event | category | flops | bytes accessed | tf_op | source)
XLA Modules:
  0.0 535.3 jit_solution(15895666665405641447)
XLA Ops:
  6.5 0.7 all-gather.3.cloned.1.call-update
  7.3 0.7 reshape.291.gain_ref
  8.0 1.7 copy.35
  9.8 1.0 copy-done.7
  10.8 1.2 copy-done.11
  12.0 1.0 copy-done.12
  13.1 1.0 copy-done.13
  14.1 1.0 copy-done.14
  15.1 44.4 %delta_chunks.1 = (bf16[1024,256]{1,0:T(8,128)(2,1)S(1)}, f32[1024,256]{1,0:T(8,128)S(1)}, bf16[2,128,256]{2,1,0:T(8,128)(2,1)S(1)}) custom-call(bf16[1024,256]{1,0:T(8,128)(2,1)S(1)} %copy-done.12, bf16[1024,256]{1,0:T(8,128)(2,1)S(1)} %copy-done.13, bf16[1024,256]{1,0:T(8,128)(2,1)S(1)} %copy-done.14, f32[1024,256]{1,0:T(8,128)S(1)} %copy-done.11, ...), custom_call_target="tpu_custom_call" | custom-call | flops 5000000000 | bytes 6000000 | tf_op jit(solution)/shard_map/delta_chunks/pallas_call | solution.py:131
  59.6 0.8 copy-done.5
  60.4 9.3 %all-gather.3.cloned.1.call-done.w_ref = bf16[2048,1152]{1,0:T(8,128)(2,1)} async-done(((bf16[256,1152]{1,0:T(8,128)(2,1)}), bf16[2048,1152]{1,0:T(8,128)(2,1)}) %all-gather.3.cloned.1.call-update) | async-done | bytes 4718608 | tf_op jit(solution)/shard_map/all_gather | solution.py:311
  69.7 1.0 copy-done.4
  70.7 1.0 copy-done.6
  71.8 1.0 copy-done.8
  72.7 42.8 %mixer.1 = (f32[128,1152]{1,0:T(8,128)S(1)}, bf16[128,1152]{1,0:T(8,128)(2,1)S(1)}) custom-call(bf16[2,128,256]{2,1,0:T(8,128)(2,1)S(1)} %get-tuple-element.10.mb_ref, bf16[1024,256]{1,0:T(8,128)(2,1)S(1)} %copy-done.6, f32[1024,256]{1,0:T(8,128)S(1)} %get-tuple-element.12.o_ref, bf16[1024,256]{1,0:T(8,128)(2,1)S(1)} %copy-done.4, ...), custom_call_target="tpu_custom_call" | custom-call | tf_op jit(solution)/shard_map/mixer/pallas_call | solution.py:269
  115.6 0.8 copy-done.2
  116.4 0.7 copy-done.9
  117.1 0.1 copy.37
  117.3 0.1 fusion.14
  117.5 0.1 copy.39
  117.6 0.1 fusion.11
  117.7 38.0 %all-gather.5.cloned.1.call-done = bf16[1024,1152]{1,0:T(8,128)(2,1)} async-done(((bf16[128,1152]{1,0:T(8,128)(2,1)}), bf16[1024,1152]{1,0:T(8,128)(2,1)}) %all-gather.5.cloned.1.call-update) | async-done | bytes 2359312 | tf_op jit(solution)/shard_map/all_gather | solution.py:322
  155.7 7.1 %gather_fusion.1 = bf16[32,128,1152]{2,1,0:T(8,128)(2,1)} fusion(bf16[8,128,1152]{2,1,0:T(8,128)(2,1)} %bitcast.48, s32[1024]{0:T(1024)S(1)} %pad_clamp_fusion.3), kind=kCustom, calls=%fused_computation.1 | custom fusion | bytes 18874496 | tf_op jit(solution)/shard_map/jit(_take)/gather | solution.py:331
  162.8 8.3 %broadcast_select_fusion = bf16[32,128,1152]{2,1,0:T(8,128)(2,1)} fusion(bf16[32,128,1152]{2,1,0:T(8,128)(2,1)} %gather_fusion.1, pred[32]{0:T(512)(128)(4,1)S(1)} %compare_and_fusion), kind=kLoop, calls=%fused_computation.5 | loop fusion | flops 4718592 | bytes 18874400 | tf_op jit(solution)/shard_map/jit(_take)/select_n | solution.py:331
  171.1 7.5 %all-to-all-start = ((bf16[32,128,1152]{2,1,0:T(8,128)(2,1)}), bf16[32,128,1152]{2,1,0:T(8,128)(2,1)}, u32[]{:S(2)}, u32[]{:S(2)}) async-start(bf16[32,128,1152]{2,1,0:T(8,128)(2,1)} %broadcast_select_fusion), calls=%async_computation | async-start | bytes 18874368 | tf_op jit(solution)/shard_map/all_to_all | solution.py:339
  178.7 0.1 eq.53
  178.8 0.1 reduce_or.9
  179.1 0.1 maximum_reduce_fusion
  179.2 0.1 select_reduce_fusion
  179.4 111.0 %all-to-all-done = bf16[32,128,1152]{2,1,0:T(8,128)(2,1)} async-done(((bf16[32,128,1152]{2,1,0:T(8,128)(2,1)}), bf16[32,128,1152]{2,1,0:T(8,128)(2,1)}, u32[]{:S(2)}, u32[]{:S(2)}) %all-to-all-start) | async-done | bytes 9437216 | tf_op jit(solution)/shard_map/all_to_all | solution.py:339
  290.4 6.9 %gather_fusion.2 = bf16[14,128,1152]{2,1,0:T(8,128)(2,1)} fusion(bf16[32,128,1152]{2,1,0:T(8,128)(2,1)} %all-to-all-done, s32[1024]{0:T(1024)S(1)} %pad_clamp_fusion.2), kind=kCustom, calls=%fused_computation.2 | custom fusion | bytes 8257592 | tf_op jit(solution)/shard_map/jit(_take)/gather | solution.py:340
  297.3 2.6 broadcast_select_fusion.2
  300.0 11.8 %fusion.2 = f32[1792,2048]{1,0:T(8,128)S(1)} fusion(bf16[1792,1152]{1,0:T(8,128)(2,1)S(1)} %bitcast.50, bf16[1,1152,2048]{2,1,0:T(8,128)(2,1)} %param.23), kind=kOutput, calls=%fused_computation.12 | convolution fusion | flops 8455716864 | bytes 23527424 | tf_op jit(solution)/shard_map/dot_general | solution.py:343
  311.8 7.4 %convolution_convert_fusion = bf16[1792,1152]{1,0:T(8,128)(2,1)} fusion(f32[1792,2048]{1,0:T(8,128)S(1)} %fusion.2, bf16[1,1024,1152]{2,1,0:T(8,128)(2,1)S(1)} %copy-done), kind=kOutput, calls=%fused_computation.7 | convolution fusion | flops 4240932864 | bytes 21168128 | tf_op jit(solution)/shard_map/dot_general | solution.py:347
  319.2 7.8 %gather_fusion.3 = bf16[32,128,1152]{2,1,0:T(8,128)(2,1)} fusion(bf16[14,128,1152]{2,1,0:T(8,128)(2,1)} %bitcast.49, s32[1024]{0:T(1024)S(1)} %pad_clamp_fusion.1), kind=kCustom, calls=%fused_computation.3 | custom fusion | bytes 18874496 | tf_op jit(solution)/shard_map/jit(_take)/gather | solution.py:352
  327.1 8.3 %broadcast_select_fusion.1 = bf16[32,128,1152]{2,1,0:T(8,128)(2,1)} fusion(bf16[32,128,1152]{2,1,0:T(8,128)(2,1)} %gather_fusion.3, pred[32]{0:T(512)(128)(4,1)S(1)} %maximum_compare_fusion), kind=kLoop, calls=%fused_computation.6 | loop fusion | flops 4718592 | bytes 18874400 | tf_op jit(solution)/shard_map/jit(_take)/select_n | solution.py:352
  335.4 12.3 %all-to-all-start.1 = ((bf16[32,128,1152]{2,1,0:T(8,128)(2,1)}), bf16[32,128,1152]{2,1,0:T(8,128)(2,1)}, u32[]{:S(2)}, u32[]{:S(2)}) async-start(bf16[32,128,1152]{2,1,0:T(8,128)(2,1)} %broadcast_select_fusion.1), calls=%async_computation.1 | async-start | bytes 18874368 | tf_op jit(solution)/shard_map/all_to_all | solution.py:351
  347.8 111.9 %all-to-all-done.1 = bf16[32,128,1152]{2,1,0:T(8,128)(2,1)} async-done(((bf16[32,128,1152]{2,1,0:T(8,128)(2,1)}), bf16[32,128,1152]{2,1,0:T(8,128)(2,1)}, u32[]{:S(2)}, u32[]{:S(2)}) %all-to-all-start.1) | async-done | bytes 9437216 | tf_op jit(solution)/shard_map/all_to_all | solution.py:351
  459.6 4.6 gather_fusion.4
  464.2 1.7 bitcast_select_fusion
  465.9 5.6 %all-to-all-start.2 = ((bf16[8,1,128,1152]{3,2,1,0:T(8,128)(2,1)}), bf16[8,1,128,1152]{3,2,1,0:T(8,128)(2,1)}, u32[]{:S(2)}, u32[]{:S(2)}) async-start(bf16[8,1,128,1152]{3,2,1,0:T(8,128)(2,1)} %bitcast_select_fusion), calls=%async_computation.2 | async-start | bytes 4718592 | tf_op jit(solution)/shard_map/all_to_all | solution.py:361
  471.6 0.2 dynamic-slice_reduce_fusion
  471.8 2.3 copy.36
  474.1 1.7 gather_fusion
  475.8 0.2 fusion.20
  476.1 49.3 %all-to-all-done.2 = bf16[8,1,128,1152]{3,2,1,0:T(8,128)(2,1)} async-done(((bf16[8,1,128,1152]{3,2,1,0:T(8,128)(2,1)}), bf16[8,1,128,1152]{3,2,1,0:T(8,128)(2,1)}, u32[]{:S(2)}, u32[]{:S(2)}) %all-to-all-start.2) | async-done | bytes 2359328 | tf_op jit(solution)/shard_map/all_to_all | solution.py:361
  525.4 2.2 fusion.1
  527.7 0.8 add_convert_fusion
  (45 shorter events, 0.5 us)
Async XLA Ops:
  6.5 305.3 %copy-start = (bf16[1,1024,1152]{2,1,0:T(8,128)(2,1)S(1)}, bf16[1,1024,1152]{2,1,0:T(8,128)(2,1)}, u32[]{:S(2)}) copy-start(bf16[1,1024,1152]{2,1,0:T(8,128)(2,1)} %param.24) | copy-start | bytes 7077892
  6.5 63.2 %all-gather.3.cloned.1.call-start = ((), (), s32[]{:S(2)}) async-start(), calls=%async_computation.3 | async-start | bytes 5308416 | tf_op jit(solution)/shard_map/all_gather | solution.py:311
  7.3 148.4 %all-gather.5.cloned.1.call-start = ((), (), s32[]{:S(2)}) async-start(), calls=%async_computation.4 | async-start | bytes 2654208 | tf_op jit(solution)/shard_map/all_gather | solution.py:322
  9.7 1.0 copy-start.7
  10.8 1.2 copy-start.11
  12.0 1.0 copy-start.12
  13.1 1.0 copy-start.13
  14.1 1.0 copy-start.14
  15.1 102.0 %copy-start.15 = (s32[256,8]{0,1:T(8,128)S(1)}, s32[256,8]{0,1:T(8,128)}, u32[]{:S(2)}) copy-start(s32[256,8]{0,1:T(8,128)} %param.25) | copy-start | bytes 24580
  59.6 0.8 copy-start.5
  69.7 1.0 copy-start.4
  70.7 1.0 copy-start.6
  71.8 1.0 copy-start.8
  115.6 0.8 copy-start.2
  116.4 0.7 copy-start.9
  171.1 119.3 %all-to-all-start = ((bf16[32,128,1152]{2,1,0:T(8,128)(2,1)}), bf16[32,128,1152]{2,1,0:T(8,128)(2,1)}, u32[]{:S(2)}, u32[]{:S(2)}) async-start(bf16[32,128,1152]{2,1,0:T(8,128)(2,1)} %broadcast_select_fusion), calls=%async_computation | async-start | bytes 18874368 | tf_op jit(solution)/shard_map/all_to_all | solution.py:339
  335.4 124.2 %all-to-all-start.1 = ((bf16[32,128,1152]{2,1,0:T(8,128)(2,1)}), bf16[32,128,1152]{2,1,0:T(8,128)(2,1)}, u32[]{:S(2)}, u32[]{:S(2)}) async-start(bf16[32,128,1152]{2,1,0:T(8,128)(2,1)} %broadcast_select_fusion.1), calls=%async_computation.1 | async-start | bytes 18874368 | tf_op jit(solution)/shard_map/all_to_all | solution.py:351
  465.9 9.9 %copy-start.10 = (bf16[128,1152]{1,0:T(8,128)(2,1)S(1)}, bf16[128,1152]{1,0:T(8,128)(2,1)}, u32[]{:S(2)}) copy-start(bf16[128,1152]{1,0:T(8,128)(2,1)} %copy-done.9) | copy-start | bytes 884740
  465.9 59.5 %all-to-all-start.2 = ((bf16[8,1,128,1152]{3,2,1,0:T(8,128)(2,1)}), bf16[8,1,128,1152]{3,2,1,0:T(8,128)(2,1)}, u32[]{:S(2)}, u32[]{:S(2)}) async-start(bf16[8,1,128,1152]{3,2,1,0:T(8,128)(2,1)} %bitcast_select_fusion), calls=%async_computation.2 | async-start | bytes 4718592 | tf_op jit(solution)/shard_map/all_to_all | solution.py:361
  471.6 56.1 %copy-start.3 = (f32[128,1152]{1,0:T(8,128)S(1)}, f32[128,1152]{1,0:T(8,128)}, u32[]{:S(2)}) copy-start(f32[128,1152]{1,0:T(8,128)} %copy-done.2) | copy-start | bytes 1769476
  471.6 56.9 %copy-start.1 = (bf16[1,1024,1152]{2,1,0:T(8,128)(2,1)S(1)}, bf16[1,1024,1152]{2,1,0:T(8,128)(2,1)}, u32[]{:S(2)}) copy-start(bf16[1,1024,1152]{2,1,0:T(8,128)(2,1)} %param.24) | copy-start | bytes 7077892
Sparse Core Ops, SparseCore 0:
  9.1 60.5 all-gather.2
  117.2 38.4 all-gather.4

commit v2 on v1

--- a/solution.py
+++ b/solution.py
@@ -290,6 +290,238 @@
     )(mb, q, o, gate, resid, gain, w_full)
 
 
+def expert_kernel(
+    normed_ref, hidden_ref, table_ref, router_ref, wgu_ref, wd_ref, out_ref,
+    spread, landed, final, own, every, leave, arrive, inner, back, home, give, take, wgu, wd,
+    fetch_s, spread_s, spread_r, every_s, every_r, leave_s, leave_r, back_s, back_r, give_s, give_r, end_s, end_r,
+):
+    seq, exp = lax.axis_index("seq"), lax.axis_index("exp")
+    seqs, exps = lax.axis_size("seq"), lax.axis_size("exp")
+    width = normed_ref.shape[1]
+    third = width // 3
+    parts = every.shape[0]
+    group = every.shape[2]
+    hidden_width = wd.shape[0]
+    core, across, along = seq % 2, (seq // 2) % 4, seq // 8
+    load_up = pltpu.make_async_copy(wgu_ref, wgu, fetch_s.at[0])
+    load_down = pltpu.make_async_copy(wd_ref, wd, fetch_s.at[1])
+    load_up.start()
+    load_down.start()
+
+    def plane(p):
+        step = p // 2
+        turn = 1 + 2 * core
+        dx = (step % 4) * turn
+        dy = ((step // 4 + step) % 4) * turn
+        return ((along + dy) % 4) * 8 + ((across + dx) % 4) * 2 + (core + p) % 2
+
+    def column(d):
+        return (exp + d) % exps
+
+    barrier = pltpu.get_barrier_semaphore()
+
+    @pl.loop(1, seqs)
+    def _(p):
+        pl.semaphore_signal(barrier, inc=1, device_id={"seq": plane(p)}, device_id_type=MESH)
+
+    @pl.loop(1, exps)
+    def _(d):
+        pl.semaphore_signal(barrier, inc=1, device_id={"exp": column(d)}, device_id_type=MESH)
+
+    row = lax.broadcasted_iota(jnp.int32, (512, 128), 0)
+    col = lax.broadcasted_iota(jnp.int32, (512, 128), 1)
+    place = (row % 16) // 4 * 32 + row // 16 == col
+    to_wire = [jnp.where(place & (row % 4 == g), 1.0, 0.0).astype(BF16) for g in range(3)]
+    row = lax.broadcasted_iota(jnp.int32, (128, 512), 0)
+    col = lax.broadcasted_iota(jnp.int32, (128, 512), 1)
+    place = (col % 16) // 4 * 32 + col // 16 == row
+    from_wire = [jnp.where(place & (col % 4 == g), 1.0, 0.0).astype(BF16) for g in range(3)]
+
+    def lay_out(rows):
+        total = mm(to_wire[0], rows[:, :third])
+        total = total + mm(to_wire[1], rows[:, third : 2 * third])
+        total = total + mm(to_wire[2], rows[:, 2 * third :])
+        spread[...] = total.astype(BF16)
+
+    def wire(peer, place, target, send, recv):
+        return pltpu.make_async_remote_copy(
+            src_ref=spread.at[pl.ds(pl.multiple_of(peer * 16, 16), 16)],
+            dst_ref=target.at[pl.ds(pl.multiple_of(place * 16, 16), 16)],
+            send_sem=send, recv_sem=recv, device_id={"seq": peer}, device_id_type=MESH)
+
+    def slots(source, target, part, peer, place, send, recv):
+        return pltpu.make_async_remote_copy(
+            src_ref=source.at[part, pl.ds(pl.multiple_of(peer * 16, 16), 16)],
+            dst_ref=target.at[part, pl.ds(pl.multiple_of(place * 16, 16), 16)],
+            send_sem=send.at[part], recv_sem=recv.at[part], device_id={"seq": peer}, device_id_type=MESH)
+
+    def settle(view, sem):
+        pltpu.make_async_copy(view, view, sem).wait()
+
+    others = (seqs - 1) * 16
+    mine = pl.ds(pl.multiple_of(seq * 16, 16), 16)
+
+    lay_out(normed_ref[...])
+    pl.semaphore_wait(barrier, seqs + exps - 2)
+
+    @pl.loop(1, seqs)
+    def _(p):
+        wire(plane(p), seq, landed, spread_s, spread_r).start()
+
+    landed[mine] = spread[mine]
+
+    table = table_ref[...]
+    lane = lax.broadcasted_iota(jnp.int32, table.shape, 1)
+    sub = lax.broadcasted_iota(jnp.int32, table.shape, 0)
+    target = jnp.sum(jnp.where(sub == exp, table, 0), axis=0, keepdims=True) // exps
+    hits = lax.broadcasted_iota(jnp.int32, (seqs, 256), 0) == target
+    before = lax.broadcasted_iota(jnp.int32, (256, 256), 0) < lax.broadcasted_iota(jnp.int32, (256, 256), 1)
+    counts = mm(jnp.where(hits, 1.0, 0.0).astype(BF16), jnp.where(before, 1.0, 0.0).astype(BF16))
+    rank = jnp.sum(jnp.where(hits, counts, 0.0), axis=0, keepdims=True)
+    goal = target.astype(F32) * 16.0 + rank
+    pick = jnp.where(lax.broadcasted_iota(jnp.int32, (512, 256), 0).astype(F32) == goal, 1.0, 0.0)
+    unpick = jnp.transpose(pick).astype(BF16)
+    pick = pick.astype(BF16)
+    ids = jnp.sum(jnp.where(lane == exp * seqs + seq, table, 0), axis=1, keepdims=True)
+    chosen = jnp.sum(jnp.where(lane == ids, 1.0, 0.0), axis=0, keepdims=True)
+    scores = mm(normed_ref[...], router_ref[...])
+    denom = jnp.sum(chosen / (1.0 + jnp.exp(-scores)), axis=1, keepdims=True)
+    here = lax.broadcasted_iota(jnp.int32, (256, 128), 0) == seq * exps + exp
+    router_col = mm(router_ref[...], jnp.where(here, 1.0, 0.0).astype(BF16)).astype(BF16)
+
+    settle(landed.at[pl.ds(0, others)], spread_r)
+    settle(spread.at[pl.ds(0, others)], spread_s)
+    for g in range(3):
+        own[:, g * third : (g + 1) * third] = mm(from_wire[g], landed[...]).astype(BF16)
+
+    def gather(part, peer, place):
+        return pltpu.make_async_remote_copy(
+            src_ref=own.at[pl.ds(pl.multiple_of(part * group, group), group)],
+            dst_ref=every.at[part, place],
+            send_sem=every_s.at[part], recv_sem=every_r.at[part], device_id={"exp": peer}, device_id_type=MESH)
+
+    @pl.loop(0, parts)
+    def _(part):
+        @pl.loop(1, exps)
+        def _(d):
+            gather(part, column(d), exp).start()
+
+        every[part, exp] = own[pl.ds(pl.multiple_of(part * group, group), group)]
+
+    @pl.loop(0, parts)
+    def _(part):
+        settle(every.at[part, pl.ds(0, exps - 1)], every_r.at[part])
+        rows = every[part].reshape(exps * group, width)
+        leave[part] = mm(pick, rows).astype(BF16)
+
+        @pl.loop(1, seqs)
+        def _(p):
+            slots(leave, arrive, part, plane(p), seq, leave_s, leave_r).start()
+
+        arrive[part, mine] = leave[part, mine]
+
+    load_up.wait()
+    load_down.wait()
+
+    @pl.loop(0, parts)
+    def _(part):
+        settle(arrive.at[part, pl.ds(0, others)], leave_r.at[part])
+        score = 1.0 / (1.0 + jnp.exp(-mm(arrive[part], router_col)))
+
+        @pl.loop(0, hidden_width // 256)
+        def _(j):
+            rows = arrive[part]
+            left = mm(rows, wgu[:, pl.ds(pl.multiple_of(j * 256, 256), 256)])
+            right = mm(rows, wgu[:, pl.ds(pl.multiple_of(hidden_width + j * 256, 256), 256)])
+            inner[:, pl.ds(pl.multiple_of(j * 256, 256), 256)] = (left / (1.0 + jnp.exp(-left)) * right).astype(BF16)
+
+        weight = jnp.concatenate([score] * 3, axis=1)
+        for g in range(3):
+            cols = pl.ds(g * third, third)
+            back[part, :, cols] = (weight * mm(inner[...], wd[:, cols])).astype(BF16)
+
+        @pl.loop(1, seqs)
+        def _(p):
+            slots(back, home, part, plane(p), seq, back_s, back_r).start()
+
+        home[part, mine] = back[part, mine]
+
+    def deliver(part, peer, place):
+        return pltpu.make_async_remote_copy(
+            src_ref=give.at[part, peer], dst_ref=take.at[part, place],
+            send_sem=give_s.at[part], recv_sem=give_r.at[part], device_id={"exp": peer}, device_id_type=MESH)
+
+    @pl.loop(0, parts)
+    def _(part):
+        settle(home.at[part, pl.ds(0, others)], back_r.at[part])
+        give[part] = mm(unpick, home[part]).astype(BF16).reshape(exps, group, width)
+
+        @pl.loop(1, exps)
+        def _(d):
+            deliver(part, column(d), exp).start()
+
+        take[part, exp] = give[part, exp]
+
+    @pl.loop(0, parts)
+    def _(part):
+        settle(take.at[part, pl.ds(0, exps - 1)], give_r.at[part])
+        own_rows = pl.ds(pl.multiple_of(part * group, group), group)
+        settle(every.at[part, pl.ds(0, exps - 1)], every_s.at[part])
+        total = take[part, 0].astype(F32)
+        for c in range(1, exps):
+            total = total + take[part, c].astype(F32)
+        own[own_rows] = total.astype(BF16)
+
+    lay_out(own[...])
+
+    @pl.loop(1, seqs)
+    def _(p):
+        wire(plane(p), seq, final, end_s, end_r).start()
+
+    final[mine] = spread[mine]
+    settle(final.at[pl.ds(0, others)], end_r)
+    scale = route_scale / denom
+    for g in range(3):
+        cols = pl.ds(g * third, third)
+        out_ref[:, cols] = (hidden_ref[:, cols] + scale * mm(from_wire[g], final[...])).astype(BF16)
+    settle(spread.at[pl.ds(0, others)], end_s)
+
+    @pl.loop(0, parts)
+    def _(part):
+        settle(leave.at[part, pl.ds(0, others)], leave_s.at[part])
+        settle(back.at[part, pl.ds(0, others)], back_s.at[part])
+        settle(give.at[part, pl.ds(0, exps - 1)], give_s.at[part])
+
+
+def experts(normed, hidden, table, router, wgu, wd, seqs, exps):
+    rows, width = normed.shape
+    parts, group = rows // seqs, seqs
+    held = seqs * 16
+    vmem = pl.BlockSpec(memory_space=pltpu.VMEM)
+    hbm = pl.BlockSpec(memory_space=pl.ANY)
+    dma = pltpu.SemaphoreType.DMA
+    slots = pltpu.VMEM((parts, held, width), BF16)
+    blocks = pltpu.VMEM((parts, exps, group, width), BF16)
+    small = pltpu.VMEM((held, width // 3), BF16)
+    return pl.pallas_call(
+        expert_kernel,
+        out_shape=jax.ShapeDtypeStruct((rows, width), BF16),
+        in_specs=[vmem] * 4 + [hbm] * 2,
+        out_specs=vmem,
+        scratch_shapes=[
+            small, small, small, pltpu.VMEM((rows, width), BF16),
+            blocks, slots, slots, pltpu.VMEM((held, wd.shape[0]), BF16), slots, slots, blocks, blocks,
+            pltpu.VMEM(wgu.shape, BF16), pltpu.VMEM(wd.shape, BF16),
+            dma((2,)), dma, dma, dma((parts,)), dma((parts,)), dma((parts,)), dma((parts,)),
+            dma((parts,)), dma((parts,)), dma((parts,)), dma((parts,)), dma, dma,
+        ],
+        compiler_params=pltpu.CompilerParams(
+            collective_id=1, has_side_effects=True, vmem_limit_bytes=56 * 2**20
+        ),
+        name="experts",
+    )(normed, hidden, table, router, wgu, wd)
+
+
 def local(
     queries,
     keys,
@@ -313,61 +545,8 @@
     hidden_state, normed = mixer(
         carried, q_lead, o_lead, out_gate, resid, norm_gain.reshape(1, -1), w_full, exp_count
     )
-    seq_index = lax.axis_index("seq")
-    exp_index = lax.axis_index("exp")
-    per_column = TOPK // exp_count
-    capacity = 2 * min(TOPK - 1, seq_count // 2)
-    layout = block_experts.reshape(seq_count, exp_count, per_column, exp_count)
-    column_pick = jnp.arange(exp_count) == exp_index
-    row_blocks = lax.all_gather(normed, "exp", axis=0, tiled=True).reshape(
-        exp_count, tok_rows, model_width
-    )
-    own_table = lax.dynamic_index_in_dim(layout, seq_index, 0, keepdims=False)
-    sent_experts = jnp.sum(jnp.where(column_pick, own_table, 0), axis=2).reshape(TOPK)
-    dest_rows = sent_experts // exp_count
-    row_match = dest_rows[None, :] == jnp.arange(seq_count)[:, None]
-    copy_block = jnp.arange(TOPK) // per_column
-    source_block = jnp.sum(jnp.where(row_match, copy_block[None, :], 0), axis=1)
-    outgoing = jnp.take(row_blocks, source_block, axis=0)
-    my_expert = seq_index * exp_count + exp_index
-    column_experts = jnp.sum(jnp.where(column_pick, layout, 0), axis=3)
-    present = jnp.any(column_experts == my_expert, axis=(1, 2))
-    slot_rank = jnp.cumsum(present.astype(jnp.int32)) - 1
-    slot_hit = present[None, :] & (slot_rank[None, :] == jnp.arange(capacity)[:, None])
-    pick_rows = jnp.sum(jnp.where(slot_hit, jnp.arange(seq_count)[None, :], 0), axis=1)
-    hidden_width = w_down.shape[1]
-    incoming_blocks = lax.all_to_all(outgoing, "seq", split_axis=0, concat_axis=0, tiled=True)
-    packed_blocks = jnp.take(incoming_blocks, pick_rows, axis=0)
-    rows_here = packed_blocks.shape[1]
-    packed = packed_blocks.reshape(capacity * rows_here, model_width)
-    gate_up = jnp.dot(packed, w_gate_up[0], preferred_element_type=jnp.float32)
-    expert_hidden = (jax.nn.silu(gate_up[:, :hidden_width]) * gate_up[:, hidden_width:]).astype(
-        jnp.bfloat16
-    )
-    expert_out = jnp.dot(expert_hidden, w_down[0], preferred_element_type=jnp.float32).astype(
-        jnp.bfloat16
-    )
-    expert_out = expert_out.reshape(capacity, rows_here, model_width)
-    returned = lax.all_to_all(
-        jnp.take(expert_out, jnp.maximum(slot_rank, 0), axis=0),
-        "seq",
-        split_axis=0,
-        concat_axis=0,
-        tiled=True,
-    )
-    per_copy = jnp.take(returned, dest_rows, axis=0).reshape(
-        exp_count, per_column, tok_rows, model_width
-    )
-    collected = lax.all_to_all(per_copy, "exp", split_axis=0, concat_axis=0, tiled=True).reshape(
-        TOPK, tok_rows, model_width
-    )
-    my_ids = lax.dynamic_index_in_dim(block_experts, my_expert, 0, keepdims=False)
-    ordered_ids = my_ids.reshape(per_column, exp_count).T.reshape(TOPK)
-    router_cols = jnp.take(router, ordered_ids, axis=1)
-    scores = jax.nn.sigmoid(jnp.dot(normed, router_cols, preferred_element_type=jnp.float32))
-    gate_weights = route_scale * scores / jnp.sum(scores, axis=1, keepdims=True)
-    combined = jnp.sum(gate_weights.T[:, :, None] * collected.astype(jnp.float32), axis=0)
-    return (hidden_state + combined).astype(jnp.bfloat16)
+    table = block_experts.reshape(seq_count, exp_count, TOPK).transpose(2, 1, 0).reshape(TOPK, -1)
+    return experts(normed, hidden_state, table, router, w_gate_up[0], w_down[0], seq_count, exp_count)
 
 
 def solution(mesh):

time: 542 us -> 304 us (0.56); the launches traced: 535 us -> 304 us
  waiting for transfers between devices: 320 us -> 11 us
  Pallas kernels: 87.3 us -> 269 us
  local copies, waits for them, and re-layouts: 44.3 us -> 10.8 us
  starting transfers between devices: 25.4 us -> 0.01 us
  other arithmetic: 25 us -> 0 us
  matrix products: 19.5 us -> 0 us
    all_to_all x3 -> x0, waiting for transfers between devices: 272 us -> none  [the longest x1 112 us: local(): lax.all_to_all(jnp.take(expert_out, jnp.maximum(slot_rank, 0), axis=0), '...]
    pallas_call x0 -> x1, Pallas kernels: none -> 182 us  [experts(): pl.pallas_call(expert_kernel, out_shape=jax.ShapeDtypeStruct((rows, width...]
    all_gather x1 -> x0, waiting for transfers between devices: 38 us -> none  [local(): lax.all_gather(normed, 'exp', axis=0, tiled=True)]
    gather x5 -> x0, local copies, waits for them, and re-layouts: 28.2 us -> none  [the longest x1 7.84 us: local(): jnp.take(expert_out, jnp.maximum(slot_rank, 0), axis=0)]
    all_to_all x3 -> x0, starting transfers between devices: 25.4 us -> none  [the longest x1 12.3 us: local(): lax.all_to_all(jnp.take(expert_out, jnp.maximum(slot_rank, 0), axis=0), '...]
    select_n x8 -> x0, other arithmetic: 21.2 us -> none  [the longest x2 8.46 us: local(): outgoing = jnp.take(row_blocks, source_block, axis=0)]
    dot_general x3 -> x0, matrix products: 19.5 us -> none  [the longest x1 11.8 us: local(): gate_up = jnp.dot(packed, w_gate_up[0], preferred_element_type=jnp.float32)]
    unnamed x35 -> x18, local copies, waits for them, and re-layouts: 14.9 us -> 8.49 us
  transfers between devices with their start and end apart: 5 -> 1, of which waited for: 5 -> 1; matrix products, arithmetic and copies ran while one was open for 2% -> 1% of each run, Pallas kernels for 8% -> 15%
where the time goes in v2:
time: 304 us
  Pallas kernels  269 us (88%)
  between operations  13.4 us (4%)
  waiting for transfers between devices  11 us (4%)
  local copies, waits for them, and re-layouts  10.8 us (4%)
    pallas_call x1, Pallas kernels, experts(): pl.pallas_call(expert_kernel, out_shape=jax.ShapeDtypeStruct((rows, width...  182 us
    pallas_call x1, Pallas kernels, delta(): pl.pallas_call(delta_kernel, grid=(rows // STEP,), out_shape=(jax.ShapeDt...  44.5 us
    pallas_call x1, Pallas kernels, mixer(): pl.pallas_call(mixer_kernel, out_shape=(jax.ShapeDtypeStruct((rows, width...  42.9 us
    all_gather x1, waiting for transfers between devices, local(): w_full = lax.all_gather(w_out, 'exp', axis=0, tiled=True)  10.3 us
    unnamed x18, local copies, waits for them, and re-layouts  8.49 us
  transfers between devices with their start and end apart: 1, of which 1 were waited for; matrix products, arithmetic and copies ran while one was open for 1% of the time, Pallas kernels for 15%

profile of v2, /device:TPU:66, one launch (start us, length us, event | category | flops | bytes accessed | tf_op | source)
XLA Modules:
  0.0 304.0 jit_solution(12060349145261634456)
XLA Ops:
  6.5 0.0 all-gather.2.cloned.1.call-start
  6.5 0.7 all-gather.2.cloned.1.call-update
  7.3 0.9 copy.16
  8.2 0.7 reshape.9.gain_ref
  8.9 0.8 reshape.10
  9.7 0.1 copy.17
  9.8 0.7 reshape.11.table_ref
  10.4 0.0 copy-start.4
  10.4 1.2 copy-done.4
  11.7 0.0 copy-start.5
  11.7 1.0 copy-done.5
  12.7 0.0 copy-start.6
  12.7 1.0 copy-done.6
  13.8 0.0 copy-start.7
  13.8 1.0 copy-done.7
  14.8 0.0 copy-start.1
  14.8 0.0 copy-start.2
  14.8 44.5 %delta_chunks.1 = (bf16[1024,256]{1,0:T(8,128)(2,1)S(1)}, f32[1024,256]{1,0:T(8,128)S(1)}, bf16[2,128,256]{2,1,0:T(8,128)(2,1)S(1)}) custom-call(bf16[1024,256]{1,0:T(8,128)(2,1)S(1)} %copy-done.5, bf16[1024,256]{1,0:T(8,128)(2,1)S(1)} %copy-done.6, bf16[1024,256]{1,0:T(8,128)(2,1)S(1)} %copy-done.7, f32[1024,256]{1,0:T(8,128)S(1)} %copy-done.4, ...), custom_call_target="tpu_custom_call" | custom-call | flops 5000000000 | bytes 6000000 | tf_op jit(solution)/shard_map/delta_chunks/pallas_call | solution.py:131
  59.3 10.3 %all-gather.2.cloned.1.call-done.w_ref = bf16[2048,1152]{1,0:T(8,128)(2,1)} async-done(((bf16[256,1152]{1,0:T(8,128)(2,1)}), bf16[2048,1152]{1,0:T(8,128)(2,1)}) %all-gather.2.cloned.1.call-update) | async-done | bytes 4718608 | tf_op jit(solution)/shard_map/all_gather | solution.py:543
  69.5 0.0 copy-done.1
  69.5 0.0 copy-done.2
  69.5 42.9 %mixer.1 = (f32[128,1152]{1,0:T(8,128)S(1)}, bf16[128,1152]{1,0:T(8,128)(2,1)S(1)}) custom-call(bf16[2,128,256]{2,1,0:T(8,128)(2,1)S(1)} %get-tuple-element.10.mb_ref, bf16[1024,256]{1,0:T(8,128)(2,1)S(1)} %get-tuple-element.11.q_ref, f32[1024,256]{1,0:T(8,128)S(1)} %get-tuple-element.12.o_ref, bf16[1024,256]{1,0:T(8,128)(2,1)S(1)} %copy-done.1, ...), custom_call_target="tpu_custom_call" | custom-call | tf_op jit(solution)/shard_map/mixer/pallas_call | solution.py:269
  112.4 0.0 copy-start
  112.5 0.8 copy-done
  113.3 0.0 copy-start.3
  113.3 0.7 copy-done.3
  114.0 181.5 %experts.1 = bf16[128,1152]{1,0:T(8,128)(2,1)} custom-call(bf16[128,1152]{1,0:T(8,128)(2,1)} %copy-done.3, f32[128,1152]{1,0:T(8,128)} %copy-done, s32[8,256]{1,0:T(8,128)} %reshape.11.table_ref, bf16[1152,256]{1,0:T(8,128)(2,1)} %router_ref.1, bf16[1152,2048]{1,0:T(8,128)(2,1)} %bitcast.7, bf16[1024,1152]{1,0:T(8,128)(2,1)} %bitcast.8), custom_call_target="tpu_custom_call" | custom-call | tf_op jit(solution)/shard_map/experts/pallas_call | solution.py:506
  295.5 1.7 copy.19
Async XLA Ops:
  6.5 63.0 %all-gather.2.cloned.1.call-start = ((), (), s32[]{:S(2)}) async-start(), calls=%async_computation | async-start | bytes 5308416 | tf_op jit(solution)/shard_map/all_gather | solution.py:543
  10.4 1.2 copy-start.4
  11.7 1.0 copy-start.5
  12.7 1.0 copy-start.6
  13.8 1.0 copy-start.7
  14.8 54.7 %copy-start.1 = (bf16[1024,256]{1,0:T(8,128)(2,1)S(1)}, bf16[1024,256]{1,0:T(8,128)(2,1)}, u32[]{:S(2)}) copy-start(bf16[1024,256]{1,0:T(8,128)(2,1)} %gate_ref.1) | copy-start | bytes 1572868
  14.8 54.7 %copy-start.2 = (bf16[128,1152]{1,0:T(8,128)(2,1)S(1)}, bf16[128,1152]{1,0:T(8,128)(2,1)}, u32[]{:S(2)}) copy-start(bf16[128,1152]{1,0:T(8,128)(2,1)} %resid_ref.1) | copy-start | bytes 884740
  112.4 0.8 copy-start
  113.3 0.7 copy-start.3
Sparse Core Ops, SparseCore 0:
  9.1 60.3 all-gather.1

commit v3 on v2

--- a/solution.py
+++ b/solution.py
@@ -11,7 +11,7 @@
 TOPK = 8
 CH = 64
 PAIR = 128
-STEP = 256
+STEP = 512
 NEAR = 8
 FAR = 4
 F32, BF16 = jnp.float32, jnp.bfloat16
@@ -65,6 +65,15 @@
     strict = same & (col < row)
     tri = jnp.where(incl, 1.0, 0.0).astype(BF16)
     eye = jnp.where(row == col, 1.0, 0.0).astype(F32)
+    first = (row // 2) == (col // 2)
+    masks = []
+    size = 2
+    while size < CH:
+        level = ((row // (2 * size)) == (col // (2 * size))) & ((row // size) != (col // size))
+        masks.append(jnp.where(level, 1.0, 0.0).astype(BF16))
+        size *= 2
+    pad = jnp.zeros((8 - heads, STEP), F32)
+    betas = jnp.transpose(jnp.concatenate([b_ref[...], pad], axis=0))
     work = {}
     for p in range(STEP // PAIR):
         rows = pl.ds(p * PAIR, PAIR)
@@ -85,38 +94,47 @@
             hs = slice(h * 128, h * 128 + 128)
             key = unit(k_ref[rows, cols].astype(F32))
             query = unit(q_ref[rows, cols].astype(F32))
-            beta = b_ref[rows, h : h + 1]
+            beta = betas[p * PAIR : p * PAIR + PAIR, h : h + 1]
             key_hat = key * grow[:, hs]
             key_inv = key * shrink[:, hs]
             key_end = key * tail[:, hs]
             query_hat = query * grow[:, hs]
             low = jnp.where(strict, dot3(key_hat, key_inv, NT) * beta, 0.0)
             score = jnp.where(incl, dot1(query_hat, key_inv, NT), 0.0)
-            inv = eye - jnp.where((row // 2 == col // 2), low, 0.0)
-            size = 2
-            while size < CH:
-                part = jnp.where((row // (2 * size) == col // (2 * size)) & (row // size != col // size), low, 0.0)
-                inv = inv - dot3(inv, dot3(part, inv))
-                size *= 2
             right = jnp.concatenate([beta * key_hat, beta * v_ref[rows, cols].astype(F32)], axis=1)
-            solved = dot3(inv, right)
-            work[p, h] = (solved, score, query_hat, key_end, total[:, hs])
+            work[p, h] = (low, right, score, query_hat, key_end, total[:, hs])
+    invs = {at: eye - jnp.where(first, work[at][0], 0.0) for at in work}
+    parts = {at: work[at][0].astype(BF16) for at in work}
+    for mask in masks:
+        held = {at: invs[at].astype(BF16) for at in work}
+        steps = {at: mm(parts[at] * mask, held[at]).astype(BF16) for at in work}
+        for at in work:
+            invs[at] = invs[at] - mm(held[at], steps[at])
+    rest = {at: eye - invs[at] - dot3(work[at][0], invs[at]) for at in work}
+    for at in work:
+        invs[at] = invs[at] + dot1(invs[at], rest[at])
+    for at in work:
+        work[at] = (dot3(invs[at], work[at][1]),) + work[at][2:]
     zero = jnp.zeros((CH, 128), F32)
-    for h in range(heads):
-        cur = state[h]
-        for p in range(STEP // PAIR):
-            solved, score, query_hat, key_end, total = work[p, h]
-            for half in range(2):
-                rs = slice(half * CH, half * CH + CH)
-                lead = dot3(jnp.concatenate([solved[rs, :128], query_hat[rs]], axis=0), cur)
-                upd = jnp.concatenate([zero, solved[rs, 128:]], axis=1) - lead[:CH]
-                out = lead[CH:] + dot1(score[rs, rs], upd)
-                at = pl.ds(p * PAIR + half * CH, CH)
+    cur = [state[h] for h in range(heads)]
+    for p in range(STEP // PAIR):
+        for half in range(2):
+            rs = slice(half * CH, half * CH + CH)
+            at = pl.ds(p * PAIR + half * CH, CH)
+            leads = []
+            for h in range(heads):
+                solved, score, query_hat, key_end, total = work[p, h]
+                leads.append(dot3(jnp.concatenate([solved[rs, :128], query_hat[rs]], axis=0), cur[h]))
+            for h in range(heads):
+                solved, score, query_hat, key_end, total = work[p, h]
+                upd = jnp.concatenate([zero, solved[rs, 128:]], axis=1) - leads[h][:CH]
+                fade = jnp.transpose(total[half * CH : half * CH + 8, :])[:, :1]
+                cur[h] = fade * cur[h] + dot3(key_end[rs], upd, TN)
+                out = leads[h][CH:] + dot1(score[rs, rs], upd)
                 qo_ref[at, h * 128 : h * 128 + 128] = out[:, :128].astype(qo_ref.dtype)
                 oo_ref[at, h * 128 : h * 128 + 128] = out[:, 128:]
-                fade = jnp.transpose(total[half * CH : half * CH + 8, :])[:, :1]
-                cur = fade * cur + dot3(key_end[rs], upd, TN)
-        state[h] = cur
+    for h in range(heads):
+        state[h] = cur[h]
 
     @pl.when(step == pl.num_programs(0) - 1)
     def _():
@@ -136,40 +154,58 @@
             jax.ShapeDtypeStruct((rows, width), F32),
             jax.ShapeDtypeStruct((heads, 128, 256), BF16),
         ),
-        in_specs=[spec, spec, spec, spec, pl.BlockSpec((STEP, heads), lambda i: (i, 0))],
+        in_specs=[spec, spec, spec, spec, pl.BlockSpec((heads, STEP), lambda i: (0, i))],
         out_specs=(spec, spec, pl.BlockSpec((heads, 128, 256), lambda i: (0, 0, 0))),
         scratch_shapes=[pltpu.VMEM((heads, 128, 256), F32)],
-        compiler_params=pltpu.CompilerParams(vmem_limit_bytes=40 * 2**20),
+        compiler_params=pltpu.CompilerParams(vmem_limit_bytes=60 * 2**20),
         cost_estimate=pl.CostEstimate(flops=5_000_000_000, bytes_accessed=6_000_000, transcendentals=0),
         name="delta_chunks",
     )(q, k, v, d, bt)
 
 
-def mixer_kernel(
-    mb_ref, q_ref, o_ref, gate_ref, resid_ref, gain_ref, w_ref, hidden_ref, normed_ref,
-    near, far, total, mixed, mix, wide, near_s, near_r, far_s, far_r, mix_s, mix_r, w_sem,
+def mixer_stage(
+    mb_ref, q_any, o_any, gate_any, resid_any, gain_ref, w_any, hidden_ref, normed_ref,
+    near, far, total, enter, mixed, mix, wide, q_ref, o_ref, gate_ref, resid_ref,
+    enter_s, near_s, near_r, far_s, far_r, mix_s, mix_r, fetch_s, share_s, share_r, ring_s, ring_r, later,
 ):
     heads = mb_ref.shape[0]
     seq, exp = lax.axis_index("seq"), lax.axis_index("exp")
-    group, slot = seq // NEAR, seq % NEAR
+    group, slot, core = seq // NEAR, seq % NEAR, seq % 2
     exps = mix.shape[0]
     rows = normed_ref.shape[0]
-    fetch = pltpu.make_async_copy(w_ref, wide, w_sem)
-    fetch.start()
-    barrier = pltpu.get_barrier_semaphore()
-    for d in range(1, NEAR):
-        peer = {"seq": group * NEAR + (slot + d) % NEAR}
-        pl.semaphore_signal(barrier, inc=1, device_id=peer, device_id_type=MESH)
-    for d in range(1, FAR):
-        peer = {"seq": ((group + d) % FAR) * NEAR + slot}
-        pl.semaphore_signal(barrier, inc=1, device_id=peer, device_id_type=MESH)
-    for d in range(1, exps):
-        pl.semaphore_signal(barrier, inc=1, device_id={"exp": (exp + d) % exps}, device_id_type=MESH)
-    pl.semaphore_wait(barrier, NEAR + FAR + exps - 3)
+    pairs = ((w_any.at[pl.ds(pl.multiple_of(core * 128, 128), 128)], wide.at[core, exp]), (q_any, q_ref), (o_any, o_ref), (gate_any, gate_ref), (resid_any, resid_ref))
+    fetches = [pltpu.make_async_copy(source, kept, fetch_s.at[i]) for i, (source, kept) in enumerate(pairs)]
+    for fetch in fetches:
+        fetch.start()
+
+    reach = (exps // 2, exps // 2 - 1)
+
+    def w_copy(way, step):
+        ahead = 1 - 2 * way
+        view = wide.at[core, (exp + exps - ahead * step) % exps]
+        return pltpu.make_async_remote_copy(
+            src_ref=view, dst_ref=view, send_sem=ring_s, recv_sem=ring_r.at[way, step],
+            device_id={"exp": (exp + exps + ahead) % exps}, device_id_type=MESH)
+
+    def share(block):
+        view = wide.at[core, block]
+        pltpu.make_async_remote_copy(
+            src_ref=view, dst_ref=view, send_sem=share_s, recv_sem=share_r,
+            device_id={"seq": seq + 1 - 2 * core}, device_id_type=MESH).start()
+
+    def advance(step):
+        for way in range(2):
+            if step <= reach[way]:
+                block = (exp + exps - (1 - 2 * way) * step) % exps
+                view = wide.at[core, block]
+                pltpu.make_async_copy(view, view, ring_r.at[way, step - 1]).wait()
+                if step < reach[way]:
+                    w_copy(way, step).start()
+                share(block)
 
     def near_copy(peer, place):
         return pltpu.make_async_remote_copy(
-            src_ref=mb_ref, dst_ref=near.at[place], send_sem=near_s.at[peer], recv_sem=near_r.at[place],
+            src_ref=mb_ref.at[peer % 2], dst_ref=near.at[place], send_sem=near_s.at[peer], recv_sem=near_r.at[place],
             device_id={"seq": group * NEAR + peer}, device_id_type=MESH)
 
     def far_copy(peer, place):
@@ -184,7 +220,14 @@
 
     for d in range(1, NEAR):
         near_copy((slot + d) % NEAR, slot).start()
-    near[slot] = mb_ref[...]
+    near[slot] = mb_ref[core]
+    for fetch in fetches:
+        fetch.wait()
+    w_copy(0, 0).start()
+    w_copy(1, 0).start()
+    share(exp)
+    for fetch in later:
+        fetch.start()
     row = lax.broadcasted_iota(jnp.int32, (128, 256), 0)
     col = lax.broadcasted_iota(jnp.int32, (128, 256), 1)
     start = jnp.where(row == col, 1.0, 0.0).astype(F32)
@@ -195,36 +238,45 @@
         lead = block[:, :128]
         return mm(lead, high) + mm(lead, low)
 
-    cur = [start] * heads
-    before = [start] * heads
+    cur, even, odd = start, start, start
     for j in range(NEAR):
         @pl.when(j != slot)
         def _():
             near_copy(j, j).wait_recv()
 
-        for h in range(heads):
-            before[h] = jnp.where(slot == j, cur[h], before[h])
-            block = near[j, h]
-            cur[h] = apply(block, cur[h]) + jnp.where(shifts, block.astype(F32), 0.0)
-    for h in range(heads):
-        total[h] = cur[h].astype(BF16)
+        if j % 2:
+            odd = jnp.where(slot // 2 == j // 2, cur, odd)
+        else:
+            even = jnp.where(slot // 2 == j // 2, cur, even)
+        block = near[j]
+        cur = apply(block, cur) + jnp.where(shifts, block.astype(F32), 0.0)
+        if j == 3:
+            advance(1)
+    total[...] = cur.astype(BF16)
     for d in range(1, FAR):
         far_copy((group + d) % FAR, group).start()
     far[group] = total[...]
-    state = [jnp.zeros((128, 128), F32)] * heads
+    advance(2)
+    state = jnp.zeros((128, 128), F32)
     for g in range(FAR):
         @pl.when(g != group)
         def _():
             far_copy(g, g).wait_recv()
 
-        for h in range(heads):
-            block = far[g, h]
-            moved = apply(block, state[h]) + block[:, 128:].astype(F32)
-            state[h] = jnp.where(g < group, moved, state[h])
-    parts = []
-    for h in range(heads):
-        entering = dot3(before[h][:, :128], state[h]) + before[h][:, 128:]
-        parts.append(split(entering))
+        block = far[g]
+        state = jnp.where(g < group, apply(block, state) + block[:, 128:].astype(F32), state)
+    first = dot3(even[:, :128], state) + even[:, 128:]
+    second = dot3(odd[:, :128], state) + odd[:, 128:]
+    enter[0] = jnp.where(core == 0, second, first).astype(BF16)
+    hand = pltpu.make_async_remote_copy(
+        src_ref=enter.at[0], dst_ref=enter.at[1], send_sem=enter_s.at[0], recv_sem=enter_s.at[1],
+        device_id={"seq": seq + 1 - 2 * core}, device_id_type=MESH)
+    hand.start()
+    advance(3)
+    mine = jnp.where(core == 0, first, second)
+    hand.wait()
+    theirs = enter[1].astype(F32)
+    parts = [split(jnp.where(core == h, mine, theirs)) for h in range(heads)]
 
     def mix_rows(peer):
         at = pl.ds(pl.multiple_of(peer * rows, rows), rows)
@@ -242,62 +294,38 @@
         mix_copy(peer, exp).start()
     mix_rows(exp)
     mix[exp] = mixed[exp]
-    fetch.wait()
+    advance(4)
+    pltpu.make_async_copy(wide.at[1 - core], wide.at[1 - core], share_r).wait()
     acc = resid_ref[...].astype(F32)
     for d in range(exps):
         source = (exp + exps - d) % exps
         if d:
             mix_copy(source, source).wait_recv()
-        wrows = pl.ds(pl.multiple_of(source * 256, 256), 256)
-        acc = acc + mm(mix[source], wide[wrows, :])
+        for h in range(heads):
+            acc = acc + mm(mix[source, :, h * 128 : h * 128 + 128], wide[h, source])
     hidden_ref[...] = acc
     scale = lax.rsqrt(jnp.mean(acc * acc, axis=-1, keepdims=True) + epsilon)
-    normed_ref[...] = (acc * scale * gain_ref[...]).astype(BF16)
+    normed_ref[...] = (acc * scale * gain_ref[...].reshape(1, -1)).astype(BF16)
     for d in range(1, NEAR):
         near_copy((slot + d) % NEAR, slot).wait_send()
     for d in range(1, FAR):
         far_copy((group + d) % FAR, group).wait_send()
     for d in range(1, exps):
         mix_copy((exp + d) % exps, exp).wait_send()
-
-
-def mixer(mb, q, o, gate, resid, gain, w_full, exps):
-    rows, width = resid.shape
-    heads = mb.shape[0]
-    vmem = pl.BlockSpec(memory_space=pltpu.VMEM)
-    dma = pltpu.SemaphoreType.DMA
-    return pl.pallas_call(
-        mixer_kernel,
-        out_shape=(
-            jax.ShapeDtypeStruct((rows, width), F32),
-            jax.ShapeDtypeStruct((rows, width), BF16),
-        ),
-        in_specs=[vmem] * 6 + [pl.BlockSpec(memory_space=pl.ANY)],
-        out_specs=(vmem, vmem),
-        scratch_shapes=[
-            pltpu.VMEM((NEAR, heads, 128, 256), BF16),
-            pltpu.VMEM((FAR, heads, 128, 256), BF16),
-            pltpu.VMEM((heads, 128, 256), BF16),
-            pltpu.VMEM((exps, rows, heads * 128), BF16),
-            pltpu.VMEM((exps, rows, heads * 128), BF16),
-            pltpu.VMEM(w_full.shape, BF16),
-            dma((NEAR,)), dma((NEAR,)), dma((FAR,)), dma((FAR,)), dma((exps,)), dma((exps,)), dma,
-        ],
-        compiler_params=pltpu.CompilerParams(
-            collective_id=0, has_side_effects=True, vmem_limit_bytes=48 * 2**20
-        ),
-        name="mixer",
-    )(mb, q, o, gate, resid, gain, w_full)
+    pltpu.make_async_copy(wide.at[core], wide.at[core], share_s).wait()
+    sent = wide.at[core, pl.ds(0, exps - 1)]
+    pltpu.make_async_copy(sent, sent, ring_s).wait()
 
 
 def expert_kernel(
-    normed_ref, hidden_ref, table_ref, router_ref, wgu_ref, wd_ref, out_ref,
-    spread, landed, final, own, every, leave, arrive, inner, back, home, give, take, wgu, wd,
+    mb_ref, q_any, o_any, gate_any, resid_any, gain_ref, w_any, table_ref, router_any, wgu_ref, wd_ref, out_ref,
+    hidden_ref, normed_ref, router_ref, near, far, total, enter, mixed, mix, wide, q_ref, o_ref, gate_ref, resid_ref,
+    enter_s, near_s, near_r, far_s, far_r, mix_s, mix_r, mixer_s, share_s, share_r, ring_s, ring_r, spread, landed, final, own, every, leave, arrive, inner, back, home, give, take, wgu, wd,
     fetch_s, spread_s, spread_r, every_s, every_r, leave_s, leave_r, back_s, back_r, give_s, give_r, end_s, end_r,
 ):
     seq, exp = lax.axis_index("seq"), lax.axis_index("exp")
     seqs, exps = lax.axis_size("seq"), lax.axis_size("exp")
-    width = normed_ref.shape[1]
+    width = out_ref.shape[1]
     third = width // 3
     parts = every.shape[0]
     group = every.shape[2]
@@ -305,15 +333,14 @@
     core, across, along = seq % 2, (seq // 2) % 4, seq // 8
     load_up = pltpu.make_async_copy(wgu_ref, wgu, fetch_s.at[0])
     load_down = pltpu.make_async_copy(wd_ref, wd, fetch_s.at[1])
-    load_up.start()
-    load_down.start()
+    load_router = pltpu.make_async_copy(router_any, router_ref, fetch_s.at[2])
 
     def plane(p):
-        step = p // 2
+        step = p % 16
         turn = 1 + 2 * core
         dx = (step % 4) * turn
         dy = ((step // 4 + step) % 4) * turn
-        return ((along + dy) % 4) * 8 + ((across + dx) % 4) * 2 + (core + p) % 2
+        return ((along + dy) % 4) * 8 + ((across + dx) % 4) * 2 + (core + p // 16) % 2
 
     def column(d):
         return (exp + d) % exps
@@ -327,6 +354,12 @@
     @pl.loop(1, exps)
     def _(d):
         pl.semaphore_signal(barrier, inc=1, device_id={"exp": column(d)}, device_id_type=MESH)
+
+    pl.semaphore_wait(barrier, seqs + exps - 2)
+    mixer_stage(
+        mb_ref, q_any, o_any, gate_any, resid_any, gain_ref, w_any, hidden_ref, normed_ref,
+        near, far, total, enter, mixed, mix, wide, q_ref, o_ref, gate_ref, resid_ref,
+        enter_s, near_s, near_r, far_s, far_r, mix_s, mix_r, mixer_s, share_s, share_r, ring_s, ring_r, (load_router, load_up, load_down))
 
     row = lax.broadcasted_iota(jnp.int32, (512, 128), 0)
     col = lax.broadcasted_iota(jnp.int32, (512, 128), 1)
@@ -362,7 +395,6 @@
     mine = pl.ds(pl.multiple_of(seq * 16, 16), 16)
 
     lay_out(normed_ref[...])
-    pl.semaphore_wait(barrier, seqs + exps - 2)
 
     @pl.loop(1, seqs)
     def _(p):
@@ -370,20 +402,25 @@
 
     landed[mine] = spread[mine]
 
-    table = table_ref[...]
+    load_router.wait()
+    count = table_ref.shape[0]
+    row = lax.broadcasted_iota(jnp.int32, (count, count), 0)
+    col = lax.broadcasted_iota(jnp.int32, (count, count), 1)
+    order = jnp.where(row == (col % seqs) * exps + col // seqs, 1.0, 0.0).astype(BF16)
+    table = mm(table_ref[...].astype(F32).astype(BF16), order, TN)
     lane = lax.broadcasted_iota(jnp.int32, table.shape, 1)
     sub = lax.broadcasted_iota(jnp.int32, table.shape, 0)
-    target = jnp.sum(jnp.where(sub == exp, table, 0), axis=0, keepdims=True) // exps
-    hits = lax.broadcasted_iota(jnp.int32, (seqs, 256), 0) == target
+    target = jnp.floor(jnp.sum(jnp.where(sub == exp, table, 0.0), axis=0, keepdims=True) / exps)
+    hits = lax.broadcasted_iota(jnp.int32, (seqs, 256), 0).astype(F32) == target
     before = lax.broadcasted_iota(jnp.int32, (256, 256), 0) < lax.broadcasted_iota(jnp.int32, (256, 256), 1)
     counts = mm(jnp.where(hits, 1.0, 0.0).astype(BF16), jnp.where(before, 1.0, 0.0).astype(BF16))
     rank = jnp.sum(jnp.where(hits, counts, 0.0), axis=0, keepdims=True)
-    goal = target.astype(F32) * 16.0 + rank
+    goal = target * 16.0 + rank
     pick = jnp.where(lax.broadcasted_iota(jnp.int32, (512, 256), 0).astype(F32) == goal, 1.0, 0.0)
     unpick = jnp.transpose(pick).astype(BF16)
     pick = pick.astype(BF16)
-    ids = jnp.sum(jnp.where(lane == exp * seqs + seq, table, 0), axis=1, keepdims=True)
-    chosen = jnp.sum(jnp.where(lane == ids, 1.0, 0.0), axis=0, keepdims=True)
+    ids = jnp.sum(jnp.where(lane == exp * seqs + seq, table, 0.0), axis=1, keepdims=True)
+    chosen = jnp.sum(jnp.where(lane.astype(F32) == ids, 1.0, 0.0), axis=0, keepdims=True)
     scores = mm(normed_ref[...], router_ref[...])
     denom = jnp.sum(chosen / (1.0 + jnp.exp(-scores)), axis=1, keepdims=True)
     here = lax.broadcasted_iota(jnp.int32, (256, 128), 0) == seq * exps + exp
@@ -394,31 +431,42 @@
     for g in range(3):
         own[:, g * third : (g + 1) * third] = mm(from_wire[g], landed[...]).astype(BF16)
 
-    def gather(part, peer, place):
-        return pltpu.make_async_remote_copy(
-            src_ref=own.at[pl.ds(pl.multiple_of(part * group, group), group)],
-            dst_ref=every.at[part, place],
-            send_sem=every_s.at[part], recv_sem=every_r.at[part], device_id={"exp": peer}, device_id_type=MESH)
-
-    @pl.loop(0, parts)
-    def _(part):
-        @pl.loop(1, exps)
-        def _(d):
-            gather(part, column(d), exp).start()
-
-        every[part, exp] = own[pl.ds(pl.multiple_of(part * group, group), group)]
-
-    @pl.loop(0, parts)
-    def _(part):
-        settle(every.at[part, pl.ds(0, exps - 1)], every_r.at[part])
-        rows = every[part].reshape(exps * group, width)
-        leave[part] = mm(pick, rows).astype(BF16)
-
-        @pl.loop(1, seqs)
-        def _(p):
-            slots(leave, arrive, part, plane(p), seq, leave_s, leave_r).start()
-
-        arrive[part, mine] = leave[part, mine]
+    def ring(part, way, step):
+        ahead = 1 - 2 * way
+        block = (exp + exps - ahead * step) % exps
+        return pltpu.make_async_remote_copy(
+            src_ref=every.at[part, block], dst_ref=every.at[part, block],
+            send_sem=every_s.at[part], recv_sem=every_r.at[part, way, step],
+            device_id={"exp": (exp + exps + ahead) % exps}, device_id_type=MESH)
+
+    def ring_wait(part, way, step):
+        block = (exp + exps - (1 - 2 * way) * (step + 1)) % exps
+        view = every.at[part, block]
+        pltpu.make_async_copy(view, view, every_r.at[part, way, step]).wait()
+
+    half = exps // 2
+    for wave in range(parts + half):
+        for part in range(parts):
+            step = wave - part
+            for way in range(2):
+                if 0 <= step < half - (part + way) % 2:
+                    if step == 0 and way == 0:
+                        every[part, exp] = own[part * group : part * group + group]
+                    if step:
+                        ring_wait(part, way, step - 1)
+                    ring(part, way, step).start()
+        part = wave - half
+        if part >= 0:
+            for way in range(2):
+                ring_wait(part, way, half - 1 - (part + way) % 2)
+            rows = every[part].reshape(exps * group, width)
+            leave[part] = mm(pick, rows).astype(BF16)
+
+            @pl.loop(1, seqs)
+            def _(p):
+                slots(leave, arrive, part, plane(p), seq, leave_s, leave_r).start()
+
+            arrive[part, mine] = leave[part, mine]
 
     load_up.wait()
     load_down.wait()
@@ -493,8 +541,9 @@
         settle(give.at[part, pl.ds(0, exps - 1)], give_s.at[part])
 
 
-def experts(normed, hidden, table, router, wgu, wd, seqs, exps):
-    rows, width = normed.shape
+def experts(mb, q, o, gate, resid, gain, w_out, table, router, wgu, wd, seqs, exps):
+    rows, width = resid.shape
+    heads = mb.shape[0]
     parts, group = rows // seqs, seqs
     held = seqs * 16
     vmem = pl.BlockSpec(memory_space=pltpu.VMEM)
@@ -503,23 +552,30 @@
     slots = pltpu.VMEM((parts, held, width), BF16)
     blocks = pltpu.VMEM((parts, exps, group, width), BF16)
     small = pltpu.VMEM((held, width // 3), BF16)
+    mixes = pltpu.VMEM((exps, rows, heads * 128), BF16)
     return pl.pallas_call(
         expert_kernel,
         out_shape=jax.ShapeDtypeStruct((rows, width), BF16),
-        in_specs=[vmem] * 4 + [hbm] * 2,
+        in_specs=[vmem] + [hbm] * 4 + [vmem, hbm, vmem] + [hbm] * 3,
         out_specs=vmem,
         scratch_shapes=[
+            pltpu.VMEM((rows, width), F32), pltpu.VMEM((rows, width), BF16), pltpu.VMEM(router.shape, BF16),
+            pltpu.VMEM((NEAR, 128, 256), BF16), pltpu.VMEM((FAR, 128, 256), BF16),
+            pltpu.VMEM((128, 256), BF16), pltpu.VMEM((2, 128, 128), BF16), mixes, mixes, pltpu.VMEM((2, exps, 128, width), BF16),
+            pltpu.VMEM(q.shape, BF16), pltpu.VMEM(o.shape, F32), pltpu.VMEM(gate.shape, BF16),
+            pltpu.VMEM(resid.shape, BF16),
+            dma((2,)), dma((NEAR,)), dma((NEAR,)), dma((FAR,)), dma((FAR,)), dma((exps,)), dma((exps,)), dma((5,)), dma, dma, dma, dma((2, exps // 2)),
             small, small, small, pltpu.VMEM((rows, width), BF16),
             blocks, slots, slots, pltpu.VMEM((held, wd.shape[0]), BF16), slots, slots, blocks, blocks,
             pltpu.VMEM(wgu.shape, BF16), pltpu.VMEM(wd.shape, BF16),
-            dma((2,)), dma, dma, dma((parts,)), dma((parts,)), dma((parts,)), dma((parts,)),
+            dma((3,)), dma, dma, dma((parts,)), dma((parts, 2, exps // 2)), dma((parts,)), dma((parts,)),
             dma((parts,)), dma((parts,)), dma((parts,)), dma((parts,)), dma, dma,
         ],
         compiler_params=pltpu.CompilerParams(
-            collective_id=1, has_side_effects=True, vmem_limit_bytes=56 * 2**20
+            collective_id=0, has_side_effects=True, vmem_limit_bytes=58 * 2**20
         ),
-        name="experts",
-    )(normed, hidden, table, router, wgu, wd)
+        name="mix_and_experts",
+    )(mb, q, o, gate, resid, gain, w_out, table, router, wgu, wd)
 
 
 def local(
@@ -539,14 +595,11 @@
 ):
     seq_count = lax.axis_size("seq")
     exp_count = lax.axis_size("exp")
-    tok_rows, model_width = resid.shape
-    w_full = lax.all_gather(w_out, "exp", axis=0, tiled=True)
-    q_lead, o_lead, carried = delta(queries, keys, values, decay_log, beta.T)
-    hidden_state, normed = mixer(
-        carried, q_lead, o_lead, out_gate, resid, norm_gain.reshape(1, -1), w_full, exp_count
+    q_lead, o_lead, carried = delta(queries, keys, values, decay_log, beta)
+    return experts(
+        carried, q_lead, o_lead, out_gate, resid, norm_gain, w_out,
+        block_experts, router, w_gate_up[0], w_down[0], seq_count, exp_count,
     )
-    table = block_experts.reshape(seq_count, exp_count, TOPK).transpose(2, 1, 0).reshape(TOPK, -1)
-    return experts(normed, hidden_state, table, router, w_gate_up[0], w_down[0], seq_count, exp_count)
 
 
 def solution(mesh):

time: 304 us -> 243 us (0.80)
  Pallas kernels: 269 us -> 239 us
  between operations: 13.4 us -> 0.01 us
  waiting for transfers between devices: 11 us -> 0 us
  local copies, waits for them, and re-layouts: 10.8 us -> 3.18 us
    pallas_call x1 -> x0, Pallas kernels: 42.9 us -> none  [mixer(): pl.pallas_call(mixer_kernel, out_shape=(jax.ShapeDtypeStruct((rows, width...]
    pallas_call x1, Pallas kernels: 182 us -> 222 us  [experts(): pl.pallas_call(expert_kernel, out_shape=jax.ShapeDtypeStruct((rows, width...]
    pallas_call x1, Pallas kernels: 44.5 us -> 17.4 us  [delta(): pl.pallas_call(delta_kernel, grid=(rows // STEP,), out_shape=(jax.ShapeDt...]
    all_gather x1 -> x0, waiting for transfers between devices: 10.3 us -> none  [local(): w_full = lax.all_gather(w_out, 'exp', axis=0, tiled=True)]
    unnamed x18 -> x2, local copies, waits for them, and re-layouts: 8.49 us -> 3.18 us
  transfers between devices with their start and end apart: 1 -> 0, of which waited for: 1 -> 0; matrix products, arithmetic and copies ran while one was open for 1% -> 0% of each run, Pallas kernels for 15% -> 0%
where the time goes in v3:
time: 243 us; the launch traced here: 242 us
  Pallas kernels  239 us (98%)
  local copies, waits for them, and re-layouts  3.18 us (1%)
    pallas_call x1, Pallas kernels, experts(): pl.pallas_call(expert_kernel, out_shape=jax.ShapeDtypeStruct((rows, width...  222 us
    pallas_call x1, Pallas kernels, delta(): pl.pallas_call(delta_kernel, grid=(rows // STEP,), out_shape=(jax.ShapeDt...  17.4 us

profile of v3, /device:TPU:66, one launch (start us, length us, event | category | flops | bytes accessed | tf_op | source)
XLA Modules:
  0.0 242.3 jit_solution(8919039222228922225)
XLA Ops:
  0.0 1.5 copy.14.table_ref
  1.5 17.4 %delta_chunks.1 = (bf16[1024,256]{1,0:T(8,128)(2,1)}, f32[1024,256]{1,0:T(8,128)}, bf16[2,128,256]{2,1,0:T(8,128)(2,1)}) custom-call(bf16[1024,256]{1,0:T(8,128)(2,1)} %q_ref.1, bf16[1024,256]{1,0:T(8,128)(2,1)} %k_ref.1, bf16[1024,256]{1,0:T(8,128)(2,1)} %v_ref.1, f32[1024,256]{1,0:T(8,128)} %d_ref.1, f32[2,1024]{1,0:T(2,128)} %b_ref.1), custom_call_target="tpu_custom_call" | custom-call | flops 5000000000 | bytes 6000000 | tf_op jit(solution)/shard_map/delta_chunks/pallas_call | solution.py:149
  18.9 221.7 %mix_and_experts.1 = bf16[128,1152]{1,0:T(8,128)(2,1)} custom-call(bf16[2,128,256]{2,1,0:T(8,128)(2,1)} %get-tuple-element.8.mb_ref, bf16[1024,256]{1,0:T(8,128)(2,1)} %get-tuple-element.9.q_any, f32[1024,256]{1,0:T(8,128)} %get-tuple-element.10.o_any, bf16[1024,256]{1,0:T(8,128)(2,1)} %gate_any.1, bf16[128,1152]{1,0:T(8,128)(2,1)} %resid_any.1, ...), custom_call_target="tpu_custom_call" | custom-call | tf_op jit(solution)/shard_map/mix_and_experts/pallas_call | solution.py:556
  240.6 1.7 copy.16

commit v4 on v3

--- a/solution.py
+++ b/solution.py
@@ -403,11 +403,11 @@
     landed[mine] = spread[mine]
 
     load_router.wait()
-    count = table_ref.shape[0]
+    count = table_ref.shape[1]
     row = lax.broadcasted_iota(jnp.int32, (count, count), 0)
     col = lax.broadcasted_iota(jnp.int32, (count, count), 1)
     order = jnp.where(row == (col % seqs) * exps + col // seqs, 1.0, 0.0).astype(BF16)
-    table = mm(table_ref[...].astype(F32).astype(BF16), order, TN)
+    table = mm(table_ref[...].astype(F32).astype(BF16), order)
     lane = lax.broadcasted_iota(jnp.int32, table.shape, 1)
     sub = lax.broadcasted_iota(jnp.int32, table.shape, 0)
     target = jnp.floor(jnp.sum(jnp.where(sub == exp, table, 0.0), axis=0, keepdims=True) / exps)
@@ -446,6 +446,18 @@
 
     half = exps // 2
     for wave in range(parts + half):
+        part = wave - half
+        if part >= 0:
+            for way in range(2):
+                ring_wait(part, way, half - 1 - (part + way) % 2)
+            rows = every[part].reshape(exps * group, width)
+            leave[part] = mm(pick, rows).astype(BF16)
+
+            @pl.loop(1, seqs)
+            def _(p):
+                slots(leave, arrive, part, plane(p), seq, leave_s, leave_r).start()
+
+            arrive[part, mine] = leave[part, mine]
         for part in range(parts):
             step = wave - part
             for way in range(2):
@@ -455,24 +467,18 @@
                     if step:
                         ring_wait(part, way, step - 1)
                     ring(part, way, step).start()
-        part = wave - half
-        if part >= 0:
-            for way in range(2):
-                ring_wait(part, way, half - 1 - (part + way) % 2)
-            rows = every[part].reshape(exps * group, width)
-            leave[part] = mm(pick, rows).astype(BF16)
-
-            @pl.loop(1, seqs)
-            def _(p):
-                slots(leave, arrive, part, plane(p), seq, leave_s, leave_r).start()
-
-            arrive[part, mine] = leave[part, mine]
 
     load_up.wait()
     load_down.wait()
 
-    @pl.loop(0, parts)
-    def _(part):
+    def send_back(part, piece, peer, start, size):
+        cols = pl.ds(start, size)
+        return pltpu.make_async_remote_copy(
+            src_ref=back.at[part, pl.ds(pl.multiple_of(peer * 16, 16), 16), cols],
+            dst_ref=home.at[part, mine, cols], send_sem=back_s.at[part], recv_sem=back_r.at[part + piece],
+            device_id={"seq": peer}, device_id_type=MESH)
+
+    def run_expert(part, pieces):
         settle(arrive.at[part, pl.ds(0, others)], leave_r.at[part])
         score = 1.0 / (1.0 + jnp.exp(-mm(arrive[part], router_col)))
 
@@ -487,38 +493,51 @@
         for g in range(3):
             cols = pl.ds(g * third, third)
             back[part, :, cols] = (weight * mm(inner[...], wd[:, cols])).astype(BF16)
-
-        @pl.loop(1, seqs)
-        def _(p):
-            slots(back, home, part, plane(p), seq, back_s, back_r).start()
+        for piece, (start, size) in enumerate(pieces):
+
+            @pl.loop(1, seqs)
+            def _(p):
+                send_back(part, piece, plane(p), start, size).start()
 
         home[part, mine] = back[part, mine]
 
-    def deliver(part, peer, place):
-        return pltpu.make_async_remote_copy(
-            src_ref=give.at[part, peer], dst_ref=take.at[part, place],
-            send_sem=give_s.at[part], recv_sem=give_r.at[part], device_id={"exp": peer}, device_id_type=MESH)
-
-    @pl.loop(0, parts)
-    def _(part):
-        settle(home.at[part, pl.ds(0, others)], back_r.at[part])
-        give[part] = mm(unpick, home[part]).astype(BF16).reshape(exps, group, width)
-
-        @pl.loop(1, exps)
-        def _(d):
-            deliver(part, column(d), exp).start()
+    def deliver(part, piece, peer, start, size):
+        cols = pl.ds(start, size)
+        return pltpu.make_async_remote_copy(
+            src_ref=give.at[part, peer, :, cols], dst_ref=take.at[part, exp, :, cols],
+            send_sem=give_s.at[part], recv_sem=give_r.at[part + piece], device_id={"exp": peer}, device_id_type=MESH)
+
+    def hand_over(part, pieces):
+        for piece, (start, size) in enumerate(pieces):
+            cols = pl.ds(start, size)
+            settle(home.at[part, pl.ds(0, others), cols], back_r.at[part + piece])
+            give[part, :, :, cols] = mm(unpick, home[part, :, cols]).astype(BF16).reshape(exps, group, size)
+
+            @pl.loop(1, exps)
+            def _(d):
+                deliver(part, piece, column(d), start, size).start()
 
         take[part, exp] = give[part, exp]
 
-    @pl.loop(0, parts)
-    def _(part):
-        settle(take.at[part, pl.ds(0, exps - 1)], give_r.at[part])
+    def add_up(part, pieces):
+        for piece, (start, size) in enumerate(pieces):
+            settle(take.at[part, pl.ds(0, exps - 1), :, pl.ds(start, size)], give_r.at[part + piece])
         own_rows = pl.ds(pl.multiple_of(part * group, group), group)
         settle(every.at[part, pl.ds(0, exps - 1)], every_s.at[part])
         total = take[part, 0].astype(F32)
         for c in range(1, exps):
             total = total + take[part, c].astype(F32)
         own[own_rows] = total.astype(BF16)
+
+    whole = ((0, width),)
+    split_last = ((0, 2 * third), (2 * third, third))
+    for stage in (run_expert, hand_over, add_up):
+
+        @pl.loop(0, parts - 1)
+        def _(part):
+            stage(part, whole)
+
+        stage(parts - 1, split_last)
 
     lay_out(own[...])
 
@@ -569,7 +588,7 @@
             blocks, slots, slots, pltpu.VMEM((held, wd.shape[0]), BF16), slots, slots, blocks, blocks,
             pltpu.VMEM(wgu.shape, BF16), pltpu.VMEM(wd.shape, BF16),
             dma((3,)), dma, dma, dma((parts,)), dma((parts, 2, exps // 2)), dma((parts,)), dma((parts,)),
-            dma((parts,)), dma((parts,)), dma((parts,)), dma((parts,)), dma, dma,
+            dma((parts,)), dma((parts + 1,)), dma((parts,)), dma((parts + 1,)), dma, dma,
         ],
         compiler_params=pltpu.CompilerParams(
             collective_id=0, has_side_effects=True, vmem_limit_bytes=58 * 2**20
@@ -598,7 +617,7 @@
     q_lead, o_lead, carried = delta(queries, keys, values, decay_log, beta)
     return experts(
         carried, q_lead, o_lead, out_gate, resid, norm_gain, w_out,
-        block_experts, router, w_gate_up[0], w_down[0], seq_count, exp_count,
+        block_experts.T, router, w_gate_up[0], w_down[0], seq_count, exp_count,
     )
 
 

time: 243 us -> 233 us (0.959); the launches traced: 242 us -> 230 us
  Pallas kernels: 239 us -> 228 us
    pallas_call x1, Pallas kernels: 222 us -> 210 us  [experts(): pl.pallas_call(expert_kernel, out_shape=jax.ShapeDtypeStruct((rows, width...]
where the time goes in v4:
time: 233 us; the launch traced here: 230 us
  Pallas kernels  228 us (98%)
    pallas_call x1, Pallas kernels, experts(): pl.pallas_call(expert_kernel, out_shape=jax.ShapeDtypeStruct((rows, width...  210 us
    pallas_call x1, Pallas kernels, delta(): pl.pallas_call(delta_kernel, grid=(rows // STEP,), out_shape=(jax.ShapeDt...  17.4 us

profile of v4, /device:TPU:66, one launch (start us, length us, event | category | flops | bytes accessed | tf_op | source)
XLA Modules:
  0.0 229.5 jit_solution(249053891580836379)
XLA Ops:
  0.0 17.4 %delta_chunks.1 = (bf16[1024,256]{1,0:T(8,128)(2,1)}, f32[1024,256]{1,0:T(8,128)}, bf16[2,128,256]{2,1,0:T(8,128)(2,1)}) custom-call(bf16[1024,256]{1,0:T(8,128)(2,1)} %q_ref.1, bf16[1024,256]{1,0:T(8,128)(2,1)} %k_ref.1, bf16[1024,256]{1,0:T(8,128)(2,1)} %v_ref.1, f32[1024,256]{1,0:T(8,128)} %d_ref.1, f32[2,1024]{1,0:T(2,128)} %b_ref.1), custom_call_target="tpu_custom_call" | custom-call | flops 5000000000 | bytes 6000000 | tf_op jit(solution)/shard_map/delta_chunks/pallas_call | solution.py:149
  17.4 210.4 %mix_and_experts.1 = bf16[128,1152]{1,0:T(8,128)(2,1)} custom-call(bf16[2,128,256]{2,1,0:T(8,128)(2,1)} %get-tuple-element.8.mb_ref, bf16[1024,256]{1,0:T(8,128)(2,1)} %get-tuple-element.9.q_any, f32[1024,256]{1,0:T(8,128)} %get-tuple-element.10.o_any, bf16[1024,256]{1,0:T(8,128)(2,1)} %gate_any.1, bf16[128,1152]{1,0:T(8,128)(2,1)} %resid_any.1, ...), custom_call_target="tpu_custom_call" | custom-call | tf_op jit(solution)/shard_map/mix_and_experts/pallas_call | solution.py:575
  227.8 1.7 copy.15

commit v5 on v4

--- a/solution.py
+++ b/solution.py
@@ -250,13 +250,11 @@
             even = jnp.where(slot // 2 == j // 2, cur, even)
         block = near[j]
         cur = apply(block, cur) + jnp.where(shifts, block.astype(F32), 0.0)
-        if j == 3:
-            advance(1)
     total[...] = cur.astype(BF16)
     for d in range(1, FAR):
         far_copy((group + d) % FAR, group).start()
     far[group] = total[...]
-    advance(2)
+    advance(1)
     state = jnp.zeros((128, 128), F32)
     for g in range(FAR):
         @pl.when(g != group)
@@ -272,7 +270,7 @@
         src_ref=enter.at[0], dst_ref=enter.at[1], send_sem=enter_s.at[0], recv_sem=enter_s.at[1],
         device_id={"seq": seq + 1 - 2 * core}, device_id_type=MESH)
     hand.start()
-    advance(3)
+    advance(2)
     mine = jnp.where(core == 0, first, second)
     hand.wait()
     theirs = enter[1].astype(F32)
@@ -292,6 +290,8 @@
         peer = (exp + d) % exps
         mix_rows(peer)
         mix_copy(peer, exp).start()
+        if d == exps // 2:
+            advance(3)
     mix_rows(exp)
     mix[exp] = mixed[exp]
     advance(4)
@@ -530,7 +530,7 @@
         own[own_rows] = total.astype(BF16)
 
     whole = ((0, width),)
-    split_last = ((0, 2 * third), (2 * third, third))
+    split_last = ((0, 2 * third), (2 * third, third - 128), (width - 128, 128))
     for stage in (run_expert, hand_over, add_up):
 
         @pl.loop(0, parts - 1)
@@ -588,7 +588,7 @@
             blocks, slots, slots, pltpu.VMEM((held, wd.shape[0]), BF16), slots, slots, blocks, blocks,
             pltpu.VMEM(wgu.shape, BF16), pltpu.VMEM(wd.shape, BF16),
             dma((3,)), dma, dma, dma((parts,)), dma((parts, 2, exps // 2)), dma((parts,)), dma((parts,)),
-            dma((parts,)), dma((parts + 1,)), dma((parts,)), dma((parts + 1,)), dma, dma,
+            dma((parts,)), dma((parts + 2,)), dma((parts,)), dma((parts + 2,)), dma, dma,
         ],
         compiler_params=pltpu.CompilerParams(
             collective_id=0, has_side_effects=True, vmem_limit_bytes=58 * 2**20

time: 233 us -> 241 us (1.034); the launches traced: 230 us -> 240 us
  Pallas kernels: 228 us -> 239 us
    pallas_call x1, Pallas kernels: 210 us -> 221 us  [experts(): pl.pallas_call(expert_kernel, out_shape=jax.ShapeDtypeStruct((rows, width...]
where the time goes in v5:
time: 241 us; the launch traced here: 240 us
  Pallas kernels  239 us (99%)
    pallas_call x1, Pallas kernels, experts(): pl.pallas_call(expert_kernel, out_shape=jax.ShapeDtypeStruct((rows, width...  221 us
    pallas_call x1, Pallas kernels, delta(): pl.pallas_call(delta_kernel, grid=(rows // STEP,), out_shape=(jax.ShapeDt...  17.4 us

profile of v5, /device:TPU:66, one launch (start us, length us, event | category | flops | bytes accessed | tf_op | source)
XLA Modules:
  0.0 240.3 jit_solution(11738627638276443670)
XLA Ops:
  0.0 17.4 %delta_chunks.1 = (bf16[1024,256]{1,0:T(8,128)(2,1)}, f32[1024,256]{1,0:T(8,128)}, bf16[2,128,256]{2,1,0:T(8,128)(2,1)}) custom-call(bf16[1024,256]{1,0:T(8,128)(2,1)} %q_ref.1, bf16[1024,256]{1,0:T(8,128)(2,1)} %k_ref.1, bf16[1024,256]{1,0:T(8,128)(2,1)} %v_ref.1, f32[1024,256]{1,0:T(8,128)} %d_ref.1, f32[2,1024]{1,0:T(2,128)} %b_ref.1), custom_call_target="tpu_custom_call" | custom-call | flops 5000000000 | bytes 6000000 | tf_op jit(solution)/shard_map/delta_chunks/pallas_call | solution.py:149
  17.4 221.1 %mix_and_experts.1 = bf16[128,1152]{1,0:T(8,128)(2,1)} custom-call(bf16[2,128,256]{2,1,0:T(8,128)(2,1)} %get-tuple-element.8.mb_ref, bf16[1024,256]{1,0:T(8,128)(2,1)} %get-tuple-element.9.q_any, f32[1024,256]{1,0:T(8,128)} %get-tuple-element.10.o_any, bf16[1024,256]{1,0:T(8,128)(2,1)} %gate_any.1, bf16[128,1152]{1,0:T(8,128)(2,1)} %resid_any.1, ...), custom_call_target="tpu_custom_call" | custom-call | tf_op jit(solution)/shard_map/mix_and_experts/pallas_call | solution.py:575
  238.6 1.7 copy.15
